TPU v7x, 512 devices: a whole 4x4x16 slice. The times are simulated.
512 devices in a mesh: wide: 64 (over z, y), narrow: 8 (over x, core).
Axes of the slice: x: 4, y: 4, z: 16, core: 2. Of those that a mesh axis runs over, the one named last changes fastest.
Arguments:
- gathered_rows: bfloat16 [64, 512, 128], P('wide', 'narrow'), may hold values from -0.59765625 to 0.59765625
- bag_counts: int32 [64, 512, 10240], P('wide', 'narrow'), may hold values from 0 to 2, as said below
- row_state: float32 [64, 512], P('wide', 'narrow'), may hold values from 100 to 10000
- cross_down: bfloat16 [512, 8192], P('narrow'), may hold values from -0.0625 to 0.0625
- cross_up: bfloat16 [512, 8192], P('narrow'), may hold values from -0.25 to 0.25
- cross_bias: float32 [8192], replicated, may hold values from -3 to 3
- upstream: bfloat16 [10240, 8192], P('wide', 'narrow'), may hold values from -6 to 6
Outputs:
- crossed: bfloat16 [10240, 8192], P('wide', 'narrow')
- new_rows: float32 [64, 512, 128], P('wide', 'narrow')
Inputs may be any that keep to these rules, and one draw needn't show every extreme that they name: `bag_counts`: each sample's bag holds each gathered row at most twice; most entries are zero.
All inputs are finite; a program needn't handle non-finite values.
Results may differ from a plain program's by a relative error of at most 0.028.
Values may be sent and summed in bfloat16 or wider, within the bound.
A program may use at most 64 MiB of HBM per device.

v0:
```python
import jax
import jax.numpy as jnp
from jax import lax
from jax.sharding import PartitionSpec as P

learning_rate = 0.2


def whole_lift(lift_term):
    return lax.psum(lift_term.astype(jnp.bfloat16), "narrow").astype(jnp.float32)


def on_device(gathered_rows, bag_counts, row_state, cross_down, cross_up, cross_bias, upstream):
    table_rows = gathered_rows[0]
    counts = bag_counts[0].astype(jnp.bfloat16)
    share_cols = upstream.shape[1]
    partial_value = lax.dot_general(
        counts, table_rows, (((0,), (0,)), ((), ())), preferred_element_type=jnp.float32
    )
    partial_value = partial_value.astype(jnp.bfloat16).astype(jnp.float32)
    pooled = lax.psum(partial_value.astype(jnp.bfloat16), "narrow")
    dense_in = lax.all_to_all(pooled, "wide", split_axis=0, concat_axis=1, tiled=True)
    grad_full = lax.all_gather(upstream, "narrow", axis=1, tiled=True)
    low = lax.dot_general(
        dense_in, cross_down, (((1,), (1,)), ((), ())), preferred_element_type=jnp.float32
    ).astype(jnp.bfloat16)
    lift_term = (
        jnp.dot(low, cross_up, preferred_element_type=jnp.float32)
        .astype(jnp.bfloat16)
        .astype(jnp.float32)
    )
    first_col = lax.axis_index("narrow") * share_cols
    dense_full = dense_in.astype(jnp.float32)
    dense_share = lax.dynamic_slice_in_dim(dense_full, first_col, share_cols, 1)
    bias_share = lax.dynamic_slice_in_dim(cross_bias, first_col, share_cols, 0)
    grad_out = grad_full.astype(jnp.float32)
    scaled = (grad_out * dense_full).astype(jnp.bfloat16)
    rank_grad = lax.dot_general(
        scaled, cross_up, (((1,), (1,)), ((), ())), preferred_element_type=jnp.float32
    ).astype(jnp.bfloat16)
    lifted_share = lax.dynamic_slice_in_dim(whole_lift(lift_term), first_col, share_cols, 1)
    crossed = (dense_share * (lifted_share + bias_share) + dense_share).astype(jnp.bfloat16)
    back_term = (
        jnp.dot(rank_grad, cross_down, preferred_element_type=jnp.float32)
        .astype(jnp.bfloat16)
        .astype(jnp.float32)
    )
    back_sum = lax.psum_scatter(
        back_term.astype(jnp.bfloat16), "narrow", scatter_dimension=1, tiled=True
    ).astype(jnp.float32)
    grad_share = (
        upstream.astype(jnp.float32) * (lifted_share + bias_share + 1.0) + back_sum
    ).astype(jnp.bfloat16)
    grad_cols = lax.all_gather(grad_share, "narrow", axis=1, tiled=True)
    table_grad = lax.all_to_all(grad_cols, "wide", split_axis=1, concat_axis=0, tiled=True)
    row_grad = jnp.dot(counts, table_grad, preferred_element_type=jnp.float32)
    state = row_state[0] + jnp.mean(row_grad * row_grad, axis=1)
    new_rows = table_rows.astype(jnp.float32) - learning_rate * row_grad / jnp.sqrt(state)[:, None]
    return (crossed, new_rows[None])


def solution(mesh):
    placed = (
        P("wide", "narrow", None),
        P("wide", "narrow", None),
        P("wide", "narrow"),
        P("narrow", None),
        P("narrow", None),
        P(),
        P("wide", "narrow"),
    )
    return jax.shard_map(
        on_device,
        mesh=mesh,
        in_specs=placed,
        out_specs=(P("wide", "narrow"), P("wide", "narrow", None)),
        check_vma=False,
    )
```

profile of v0, /device:TPU:1, one launch (start us, length us, event | category | flops | bytes accessed | tf_op | source)
XLA Modules:
  0.0 543.1 jit_solution(10599563114363686089)
XLA Ops:
  7.2 0.0 all-reduce.3.cloned.1.call-start
  7.2 4.2 convolution_convert_fusion
  11.5 0.0 all-reduce.3.cloned.1.call-update
  11.5 86.4 %all-reduce.3.cloned.1.call-done = bf16[64,160,128]{2,1,0:T(8,128)(2,1)} async-done(((bf16[64,160,128]{2,1,0:T(8,128)(2,1)}), bf16[64,160,128]{2,1,0:T(8,128)(2,1)}) %all-reduce.3.cloned.1.call-update) | async-done | bytes 2621456 | tf_op jit(solution)/shard_map/psum | solution.py:21
  97.9 15.5 %all-to-all-start = ((bf16[64,160,128]{2,1,0:T(8,128)(2,1)}), bf16[64,160,128]{2,1,0:T(8,128)(2,1)}, u32[]{:S(2)}, u32[]{:S(2)}) async-start(bf16[64,160,128]{2,1,0:T(8,128)(2,1)} %all-reduce.3.cloned.1.call-done), calls=%async_computation | async-start | bytes 5242880 | tf_op jit(solution)/shard_map/all_to_all | solution.py:22
  113.4 0.0 all-gather.3.cloned.1.call-start
  113.5 0.7 all-gather.3.cloned.1.call-update
  114.2 0.0 all-reduce.5.cloned.1.call-start
  114.2 114.7 %all-to-all-done = bf16[64,160,128]{2,1,0:T(8,128)(2,1)} async-done(((bf16[64,160,128]{2,1,0:T(8,128)(2,1)}), bf16[64,160,128]{2,1,0:T(8,128)(2,1)}, u32[]{:S(2)}, u32[]{:S(2)}) %all-to-all-start) | async-done | bytes 2621472 | tf_op jit(solution)/shard_map/all_to_all | solution.py:22
  228.9 6.2 %convolution_convert_fusion.2 = bf16[160,8192]{1,0:T(8,128)(2,1)} fusion(bf16[64,8192]{1,0:T(8,128)(2,1)S(1)} %copy-done, bf16[64,8192]{1,0:T(8,128)(2,1)S(1)} %copy-done.2, bf16[64,160,128]{2,1,0:T(8,128)(2,1)} %all-to-all-done), kind=kOutput, calls=%fused_computation.2 | convolution fusion | flops 336865280 | bytes 7340032 | tf_op jit(solution)/shard_map/dot_general | solution.py:28
  235.1 0.0 reduce-scatter.2.cloned.1.call-start
  235.2 0.0 all-gather.3.cloned.1.call-done
  235.2 6.9 %convolution_convert_fusion.1 = bf16[160,8192]{1,0:T(8,128)(2,1)} fusion(bf16[64,8192]{1,0:T(8,128)(2,1)S(1)} %copy-done.2, bf16[64,8192]{1,0:T(8,128)(2,1)S(1)} %copy-done, bf16[160,8192]{1,0:T(8,128)(2,1)} %all-gather.3.cloned.1.call-done, bf16[64,160,128]{2,1,0:T(8,128)(2,1)} %all-to-all-done), kind=kOutput, calls=%fused_computation.1 | convolution fusion | flops 342108160 | bytes 9961472 | tf_op jit(solution)/shard_map/dot_general | solution.py:44
  242.1 0.0 all-gather.5.cloned.1.call-start
  242.2 4.6 bitcast_convert_fusion
  246.9 68.3 %all-reduce.5.cloned.1.call-done = bf16[160,8192]{1,0:T(8,128)(2,1)} async-done(((bf16[160,8192]{1,0:T(8,128)(2,1)}), bf16[160,8192]{1,0:T(8,128)(2,1)}) %all-reduce.5.cloned.1.call-update) | async-done | bytes 2621456 | tf_op jit(solution)/shard_map/psum | solution.py:10
  315.1 44.8 %reduce-scatter.2.cloned.1.call-done = bf16[160,1024]{1,0:T(8,128)(2,1)} async-done(((bf16[160,8192]{1,0:T(8,128)(2,1)}), bf16[160,1024]{1,0:T(8,128)(2,1)}) %reduce-scatter.2.cloned.1.call-update) | async-done | bytes 327696 | tf_op jit(solution)/shard_map/reduce_scatter | solution.py:48
  359.9 2.4 add_convert_fusion
  362.3 0.0 all-gather.5.cloned.1.call-update
  362.3 35.2 %all-gather.5.cloned.1.call-done = bf16[160,8192]{1,0:T(8,128)(2,1)} async-done(((bf16[160,1024]{1,0:T(8,128)(2,1)}), bf16[160,8192]{1,0:T(8,128)(2,1)}) %all-gather.5.cloned.1.call-update) | async-done | bytes 2621456 | tf_op jit(solution)/shard_map/all_gather | solution.py:54
  397.5 2.2 copy_bitcast_fusion
  399.7 135.4 %all_to_all.38 = bf16[160,64,128]{2,0,1:T(8,128)(2,1)S(1)} all-to-all(bf16[160,64,128]{2,0,1:T(8,128)(2,1)S(1)} %copy_bitcast_fusion), channel_id=1, replica_groups=mesh['wide'=64,'narrow'=8] {'wide'}, dimensions={1} | all-to-all | bytes 5242880 | tf_op jit(solution)/shard_map/all_to_all | solution.py:55
  535.1 0.7 multiply_reduce_fusion
  535.9 0.7 fusion.16
  (17 shorter events, 0.1 us)
Async XLA Ops:
  7.2 221.7 %copy-start = (bf16[64,8192]{1,0:T(8,128)(2,1)S(1)}, bf16[64,8192]{1,0:T(8,128)(2,1)}, u32[]{:S(2)}) copy-start(bf16[64,8192]{1,0:T(8,128)(2,1)} %param.11) | copy-start | bytes 3145732
  7.2 90.7 %all-reduce.3.cloned.1.call-start = ((), (), s32[]{:S(2)}) async-start(), calls=%async_computation.3 | async-start | bytes 5242880 | tf_op jit(solution)/shard_map/psum | solution.py:21
  11.5 217.4 %copy-start.2 = (bf16[64,8192]{1,0:T(8,128)(2,1)S(1)}, bf16[64,8192]{1,0:T(8,128)(2,1)}, u32[]{:S(2)}) copy-start(bf16[64,8192]{1,0:T(8,128)(2,1)} %param.10) | copy-start | bytes 3145732
  97.9 131.0 %all-to-all-start = ((bf16[64,160,128]{2,1,0:T(8,128)(2,1)}), bf16[64,160,128]{2,1,0:T(8,128)(2,1)}, u32[]{:S(2)}, u32[]{:S(2)}) async-start(bf16[64,160,128]{2,1,0:T(8,128)(2,1)} %all-reduce.3.cloned.1.call-done), calls=%async_computation | async-start | bytes 5242880 | tf_op jit(solution)/shard_map/all_to_all | solution.py:22
  113.4 121.8 %all-gather.3.cloned.1.call-start = ((), (), s32[]{:S(2)}) async-start(), calls=%async_computation.5 | async-start | bytes 2949120 | tf_op jit(solution)/shard_map/all_gather | solution.py:23
  114.2 201.0 %all-reduce.5.cloned.1.call-start = ((), (), s32[]{:S(2)}) async-start(), calls=%async_computation.4 | async-start | bytes 5242880 | tf_op jit(solution)/shard_map/psum | solution.py:10
  235.1 124.8 %reduce-scatter.2.cloned.1.call-start = ((), (), s32[]{:S(2)}) async-start(), calls=%async_computation.6 | async-start | bytes 2949120 | tf_op jit(solution)/shard_map/reduce_scatter | solution.py:48
  242.1 155.3 %all-gather.5.cloned.1.call-start = ((), (), s32[]{:S(2)}) async-start(), calls=%async_computation.7 | async-start | bytes 2949120 | tf_op jit(solution)/shard_map/all_gather | solution.py:54
  242.2 117.7 %copy-start.3 = (bf16[160,1024]{1,0:T(8,128)(2,1)S(1)}, bf16[160,1024]{1,0:T(8,128)(2,1)}, u32[]{:S(2)}) copy-start(bf16[160,1024]{1,0:T(8,128)(2,1)} %param.13) | copy-start | bytes 983044
  242.2 117.7 %dynamic-slice-start = ((f32[8192]{0:T(1024)}, s32[]{:T(128)}), f32[1024]{0:T(1024)S(1)}, s32[]{:S(2)}) async-start(f32[8192]{0:T(1024)} %param.12, s32[]{:T(128)} %select_n.2), calls=%async_computation.8 | async-start | bytes 8704 | tf_op jit(solution)/shard_map/dynamic_slice | solution.py:35
  399.7 135.5 %copy-start.1 = (s32[1,64,10240]{2,1,0:T(8,128)S(1)}, s32[1,64,10240]{2,1,0:T(8,128)}, u32[]{:S(2)}) copy-start(s32[1,64,10240]{2,1,0:T(8,128)} %param.8) | copy-start | bytes 7864324
  535.1 0.7 copy-start.5
  535.1 0.7 copy-start.4
Sparse Core Ops, SparseCore 0:
  11.6 86.2 all-reduce.2
  116.4 34.9 all-gather.2
  235.2 79.8 all-reduce.4
  317.8 42.0 reduce-scatter.1
  362.4 35.0 all-gather.4
where the time goes:
time: 545 us; the launch traced here: 543 us
  waiting for transfers between devices  350 us (64%)
  blocking collectives  135 us (25%)
  matrix products  18.1 us (3%)
  starting transfers between devices  15.7 us (3%)
  between operations  13.9 us (3%)
  other arithmetic  7.74 us (1%)
    all_to_all x1, blocking collectives, on_device(): lax.all_to_all(grad_cols, 'wide', split_axis=1, concat_axis=0, tiled=True)  135 us
    all_to_all x1, waiting for transfers between devices, on_device(): lax.all_to_all(pooled, 'wide', split_axis=0, concat_axis=1, tiled=True)  115 us
    psum x1, waiting for transfers between devices, on_device(): pooled = lax.psum(partial_value.astype(jnp.bfloat16), 'narrow')  86.4 us
    psum x1, waiting for transfers between devices, whole_lift(): lax.psum(lift_term.astype(jnp.bfloat16), 'narrow').astype(jnp.float32)  68.3 us
    reduce_scatter x1, waiting for transfers between devices, on_device(): lax.psum_scatter(back_term.astype(jnp.bfloat16), 'narrow', scatter_dimens...  44.8 us
    all_gather x1, waiting for transfers between devices, on_device(): grad_cols = lax.all_gather(grad_share, 'narrow', axis=1, tiled=True)  35.2 us
    all_to_all x1, starting transfers between devices, on_device(): lax.all_to_all(pooled, 'wide', split_axis=0, concat_axis=1, tiled=True)  15.5 us
  transfers between devices with their start and end apart: 6, of which 5 were waited for; matrix products, arithmetic and copies ran while one was open for 3% of the time, Pallas kernels for 0%

commit v1 on v0

v1 whole, which is shorter than its diff:
```python
import jax
import jax.numpy as jnp
from jax import lax
from jax.sharding import PartitionSpec as P

learning_rate = 0.2


def on_device(gathered_rows, bag_counts, row_state, cross_down, cross_up, cross_bias, upstream):
    f32, bf16 = jnp.float32, jnp.bfloat16
    n = lax.axis_size("narrow")
    wide = lax.axis_size("wide")
    rows_dev, emb = gathered_rows.shape[1:]
    batch = bag_counts.shape[2]
    block, cols = upstream.shape
    sub = block // n
    counts = bag_counts[0].astype(bf16).reshape(rows_dev, wide, n, sub).transpose(2, 0, 1, 3)
    counts = lax.all_to_all(
        counts.reshape(n, rows_dev, wide * sub), "narrow", split_axis=0, concat_axis=0, tiled=True
    ).reshape(n * rows_dev, wide * sub)
    rows_all = lax.all_gather(gathered_rows[0], "narrow", axis=0, tiled=True)
    rank_dev = cross_down.shape[0]
    both = jnp.stack([cross_down, cross_up]).reshape(2 * rank_dev, n, cols).transpose(1, 0, 2)
    both = lax.all_to_all(both, "narrow", split_axis=0, concat_axis=0, tiled=True)
    down = both[:, :rank_dev].reshape(n * rank_dev, cols)
    up = both[:, rank_dev:].reshape(n * rank_dev, cols)

    pooled = lax.dot_general(
        counts, rows_all, (((0,), (0,)), ((), ())), preferred_element_type=f32
    ).astype(bf16)
    pooled = lax.all_to_all(
        pooled.reshape(wide, sub, emb), "wide", split_axis=0, concat_axis=0, tiled=True
    )
    dense = lax.all_to_all(pooled, "narrow", split_axis=0, concat_axis=0, tiled=True)
    dense = dense.reshape(n, wide // n, sub, emb).transpose(0, 2, 1, 3).reshape(block, cols)
    dense_f = dense.astype(f32)
    grad_f = upstream.astype(f32)
    scaled = (grad_f * dense_f).astype(bf16)
    contract_cols = (((1,), (1,)), ((), ()))
    low = lax.dot_general(dense, down, contract_cols, preferred_element_type=f32)
    rank_grad = lax.dot_general(scaled, up, contract_cols, preferred_element_type=f32)
    ranks = lax.psum(jnp.concatenate([low, rank_grad], axis=1).astype(bf16), "narrow")
    low, rank_grad = jnp.split(ranks, 2, axis=1)
    lifted = jnp.dot(low, up, preferred_element_type=f32)
    back = jnp.dot(rank_grad, down, preferred_element_type=f32)
    bias = lax.dynamic_slice_in_dim(cross_bias, lax.axis_index("narrow") * cols, cols, 0)
    crossed = (dense_f * (lifted + bias) + dense_f).astype(bf16)
    grad = (grad_f * (lifted + bias + 1.0) + back).astype(bf16)
    grad = grad.reshape(n, sub, wide // n, emb).transpose(0, 2, 1, 3)
    grad = lax.all_to_all(grad, "narrow", split_axis=0, concat_axis=0, tiled=True)
    grad = lax.all_to_all(
        grad.reshape(wide, sub, emb), "wide", split_axis=0, concat_axis=0, tiled=True
    ).reshape(wide * sub, emb)
    row_grad = jnp.dot(counts, grad, preferred_element_type=f32)
    row_grad = lax.psum_scatter(row_grad, "narrow", scatter_dimension=0, tiled=True)
    state = row_state[0] + jnp.mean(row_grad * row_grad, axis=1)
    new_rows = (
        gathered_rows[0].astype(f32) - learning_rate * row_grad / jnp.sqrt(state)[:, None]
    )
    return (crossed, new_rows[None])


def solution(mesh):
    placed = (
        P("wide", "narrow", None),
        P("wide", "narrow", None),
        P("wide", "narrow"),
        P("narrow", None),
        P("narrow", None),
        P(),
        P("wide", "narrow"),
    )
    return jax.shard_map(
        on_device,
        mesh=mesh,
        in_specs=placed,
        out_specs=(P("wide", "narrow"), P("wide", "narrow", None)),
        check_vma=False,
    )
```

time: 545 us -> 306 us (0.56)
  waiting for transfers between devices: 350 us -> 113 us
  local copies, waits for them, and re-layouts: 2.24 us -> 23.5 us
  matrix products: 18.1 us -> 4.65 us
  blocking collectives: 135 us -> 125 us
  starting transfers between devices: 15.7 us -> 21.6 us
    all_to_all x1 -> x3, waiting for transfers between devices: 115 us -> 20.2 us  [the longest x1 13.8 us: on_device(): lax.all_to_all(counts.reshape(n, rows_dev, wide * sub), 'narrow', split_a...]
    psum x2 -> x1, waiting for transfers between devices: 155 us -> 63.5 us  [on_device(): lax.psum(jnp.concatenate([low, rank_grad], axis=1).astype(bf16), 'narrow')]
    reduce_scatter x1 -> x0, waiting for transfers between devices: 44.8 us -> none  [on_device(): lax.psum_scatter(back_term.astype(jnp.bfloat16), 'narrow', scatter_dimens...]
    all_to_all x1 -> x3, blocking collectives: 135 us -> 91.9 us  [the longest x1 39.9 us: on_device(): lax.all_to_all(pooled.reshape(wide, sub, emb), 'wide', split_axis=0, conc...]
    all_gather x2 -> x0, waiting for transfers between devices: 35.2 us -> none  [the longest x1 35.2 us: on_device(): grad_cols = lax.all_gather(grad_share, 'narrow', axis=1, tiled=True)]
    all_gather x0 -> x1, blocking collectives: none -> 33 us  [on_device(): rows_all = lax.all_gather(gathered_rows[0], 'narrow', axis=0, tiled=True)]
    unnamed x5 -> x3, waiting for transfers between devices: 0.76 us -> 29.1 us
    dot_general x4 -> x6, matrix products: 18.1 us -> 4.65 us  [the longest x1 2.19 us: on_device(): lifted = jnp.dot(low, up, preferred_element_type=f32)]
  transfers between devices with their start and end apart: 6 -> 5, of which waited for: 5 -> 4; matrix products, arithmetic and copies ran while one was open for 3% -> 2% of each run, Pallas kernels for 0% -> 0%
where the time goes in v1:
time: 306 us; the launch traced here: 304 us
  blocking collectives  125 us (41%)
  waiting for transfers between devices  113 us (37%)
  local copies, waits for them, and re-layouts  23.5 us (8%)
  starting transfers between devices  21.6 us (7%)
  between operations  14.2 us (5%)
  matrix products  4.65 us (2%)
    psum x1, waiting for transfers between devices, on_device(): lax.psum(jnp.concatenate([low, rank_grad], axis=1).astype(bf16), 'narrow')  63.5 us
    all_to_all x1, blocking collectives, on_device(): lax.all_to_all(pooled.reshape(wide, sub, emb), 'wide', split_axis=0, conc...  39.9 us
    all_to_all x1, blocking collectives, on_device(): lax.all_to_all(grad.reshape(wide, sub, emb), 'wide', split_axis=0, concat...  39.8 us
    all_gather x1, blocking collectives, on_device(): rows_all = lax.all_gather(gathered_rows[0], 'narrow', axis=0, tiled=True)  33 us
    unnamed x3, waiting for transfers between devices  29.1 us
    all_to_all x1, waiting for transfers between devices, on_device(): lax.all_to_all(counts.reshape(n, rows_dev, wide * sub), 'narrow', split_a...  13.8 us
    all_to_all x1, blocking collectives, on_device(): lax.all_to_all(grad, 'narrow', split_axis=0, concat_axis=0, tiled=True)  12.1 us
    all_to_all x1, starting transfers between devices, on_device(): lax.all_to_all(counts.reshape(n, rows_dev, wide * sub), 'narrow', split_a...  10.5 us
  transfers between devices with their start and end apart: 5, of which 4 were waited for; matrix products, arithmetic and copies ran while one was open for 2% of the time, Pallas kernels for 0%

profile of v1, /device:TPU:1, one launch (start us, length us, event | category | flops | bytes accessed | tf_op | source)
XLA Modules:
  0.0 304.5 jit_solution(13100650708750752434)
XLA Ops:
  7.2 1.9 convert_element_type.29
  9.0 2.6 copy.29
  11.7 3.9 %convert_element_type.30 = bf16[64,64,8,20]{0,3,2,1:T(8,128)(2,1)S(1)} reshape(bf16[1,64,10240]{1,2,0:T(8,128)(2,1)} %copy.29) | data formatting | bytes 2621440 | tf_op jit(solution)/shard_map/convert_element_type | solution.py:17
  15.5 1.9 copy.30
  17.4 4.4 %copy.31 = bf16[8,64,1280]{2,1,0:T(8,128)(2,1)} copy(bf16[8,64,1280]{1,0,2:T(8,128)(2,1)} %bitcast.60) | data formatting | bytes 2621440 | tf_op jit(solution)/shard_map/reshape | solution.py:19
  21.9 10.5 %all-to-all-start = ((bf16[8,64,1280]{2,1,0:T(8,128)(2,1)}), bf16[8,64,1280]{2,1,0:T(8,128)(2,1)S(1)}, u32[]{:S(2)}, u32[]{:S(2)}) async-start(bf16[8,64,1280]{2,1,0:T(8,128)(2,1)} %copy.31), calls=%async_computation | async-start | bytes 2621440 | tf_op jit(solution)/shard_map/all_to_all | solution.py:18
  32.6 1.4 copy.41
  34.0 2.5 copy.33
  36.4 13.8 %all-to-all-done = bf16[8,64,1280]{2,1,0:T(8,128)(2,1)S(1)} async-done(((bf16[8,64,1280]{2,1,0:T(8,128)(2,1)}), bf16[8,64,1280]{2,1,0:T(8,128)(2,1)S(1)}, u32[]{:S(2)}, u32[]{:S(2)}) %all-to-all-start) | async-done | bytes 1310752 | tf_op jit(solution)/shard_map/all_to_all | solution.py:18
  50.3 5.1 %all-to-all-start.3 = ((bf16[8,128,1024]{2,1,0:T(8,128)(2,1)}), bf16[8,128,1024]{2,1,0:T(8,128)(2,1)}, u32[]{:S(2)}, u32[]{:S(2)}) async-start(bf16[8,128,1024]{2,1,0:T(8,128)(2,1)} %copy.33), calls=%async_computation.3 | async-start | bytes 4194304 | tf_op jit(solution)/shard_map/all_to_all | solution.py:24
  55.4 33.0 %all-gather = bf16[1,512,128]{2,1,0:T(8,128)(2,1)S(1)} all-gather(bf16[1,64,128]{2,1,0:T(8,128)(2,1)S(1)} %copy-done.6), channel_id=2, replica_groups=mesh['wide'=64,'narrow'=8] {'narrow'}, dimensions={1}, use_global_device_ids=true | all-gather | bytes 147456 | tf_op jit(solution)/shard_map/all_gather | solution.py:21
  89.0 39.9 %all_to_all.30 = bf16[64,20,128]{2,1,0:T(8,128)(2,1)} all-to-all(bf16[64,20,128]{2,1,0:T(8,128)(2,1)S(1)} %reshape.52), channel_id=1, replica_groups=mesh['wide'=64,'narrow'=8] {'wide'}, dimensions={0} | all-to-all | bytes 655360 | tf_op jit(solution)/shard_map/all_to_all | solution.py:31
  128.9 6.0 %all-to-all-start.2 = ((bf16[64,20,128]{2,1,0:T(8,128)(2,1)}), bf16[64,20,128]{2,1,0:T(8,128)(2,1)}, u32[]{:S(2)}, u32[]{:S(2)}) async-start(bf16[64,20,128]{2,1,0:T(8,128)(2,1)} %all_to_all.30), calls=%async_computation.2 | async-start | bytes 786432 | tf_op jit(solution)/shard_map/all_to_all | solution.py:34
  134.9 1.8 fusion.14
  136.7 6.4 %all-to-all-done.2 = bf16[64,20,128]{2,1,0:T(8,128)(2,1)} async-done(((bf16[64,20,128]{2,1,0:T(8,128)(2,1)}), bf16[64,20,128]{2,1,0:T(8,128)(2,1)}, u32[]{:S(2)}, u32[]{:S(2)}) %all-to-all-start.2) | async-done | bytes 327712 | tf_op jit(solution)/shard_map/all_to_all | solution.py:34
  143.1 1.1 copy.32
  145.4 0.8 pad_maximum_fusion.1
  147.0 63.5 %all-reduce.2.cloned.1.call-done = bf16[160,1024]{1,0:T(8,128)(2,1)} async-done(((bf16[160,1024]{1,0:T(8,128)(2,1)}), bf16[160,1024]{1,0:T(8,128)(2,1)}) %all-reduce.2.cloned.1.call-update) | async-done | bytes 327696 | tf_op jit(solution)/shard_map/psum | solution.py:42
  210.4 2.2 fusion.3
  213.0 12.1 %all_to_all.31 = bf16[8,8,20,128]{3,1,2,0:T(8,128)(2,1)S(1)} all-to-all(bf16[8,8,20,128]{3,1,2,0:T(8,128)(2,1)S(1)} %bitcast.70), channel_id=1, replica_groups=mesh['wide'=64,'narrow'=8] {'narrow'}, dimensions={0} | all-to-all | bytes 655360 | tf_op jit(solution)/shard_map/all_to_all | solution.py:50
  225.5 39.8 %all_to_all.32 = bf16[64,20,128]{2,1,0:T(8,128)(2,1)S(1)} all-to-all(bf16[64,20,128]{2,1,0:T(8,128)(2,1)S(1)} %copy.36), channel_id=1, replica_groups=mesh['wide'=64,'narrow'=8] {'wide'}, dimensions={0} | all-to-all | bytes 655360 | tf_op jit(solution)/shard_map/all_to_all | solution.py:51
  266.0 0.8 copy.38
  267.0 29.0 %reduce-scatter.4.cloned.1.call-done = f32[64,128]{1,0:T(8,128)} async-done(((f32[512,128]{1,0:T(8,128)}), f32[64,128]{1,0:T(8,128)}) %reduce-scatter.4.cloned.1.call-update) | async-done | bytes 32784
  296.0 0.8 copy.39
  (38 shorter events, 5.0 us)
Async XLA Ops:
  21.9 10.5 %copy-start.3 = (bf16[64,8192]{1,0:T(8,128)(2,1)S(1)}, bf16[64,8192]{1,0:T(8,128)(2,1)}, u32[]{:S(2)}) copy-start(bf16[64,8192]{1,0:T(8,128)(2,1)} %param.11) | copy-start | bytes 3145732
  21.9 10.5 %copy-start.4 = (bf16[64,8192]{1,0:T(8,128)(2,1)S(1)}, bf16[64,8192]{1,0:T(8,128)(2,1)}, u32[]{:S(2)}) copy-start(bf16[64,8192]{1,0:T(8,128)(2,1)} %param.10) | copy-start | bytes 3145732
  21.9 28.4 %all-to-all-start = ((bf16[8,64,1280]{2,1,0:T(8,128)(2,1)}), bf16[8,64,1280]{2,1,0:T(8,128)(2,1)S(1)}, u32[]{:S(2)}, u32[]{:S(2)}) async-start(bf16[8,64,1280]{2,1,0:T(8,128)(2,1)} %copy.31), calls=%async_computation | async-start | bytes 2621440 | tf_op jit(solution)/shard_map/all_to_all | solution.py:18
  36.4 18.9 %copy-start.6 = (bf16[1,64,128]{2,1,0:T(8,128)(2,1)S(1)}, bf16[1,64,128]{2,1,0:T(8,128)(2,1)}, u32[]{:S(2)}) copy-start(bf16[1,64,128]{2,1,0:T(8,128)(2,1)} %param.7) | copy-start | bytes 49156
  50.3 38.7 %all-to-all-start.3 = ((bf16[8,128,1024]{2,1,0:T(8,128)(2,1)}), bf16[8,128,1024]{2,1,0:T(8,128)(2,1)}, u32[]{:S(2)}, u32[]{:S(2)}) async-start(bf16[8,128,1024]{2,1,0:T(8,128)(2,1)} %copy.33), calls=%async_computation.3 | async-start | bytes 4194304 | tf_op jit(solution)/shard_map/all_to_all | solution.py:24
  128.9 14.2 %all-to-all-start.2 = ((bf16[64,20,128]{2,1,0:T(8,128)(2,1)}), bf16[64,20,128]{2,1,0:T(8,128)(2,1)}, u32[]{:S(2)}, u32[]{:S(2)}) async-start(bf16[64,20,128]{2,1,0:T(8,128)(2,1)} %all_to_all.30), calls=%async_computation.2 | async-start | bytes 786432 | tf_op jit(solution)/shard_map/all_to_all | solution.py:34
  134.9 75.5 %all-reduce.2.cloned.1.call-start = ((), (), s32[]{:S(2)}) async-start(), calls=%async_computation.7 | async-start | bytes 655360 | tf_op jit(solution)/shard_map/psum | solution.py:42
  143.1 1.8 copy-start.1
  144.2 0.7 copy-start
  146.2 149.8 %reduce-scatter.4.cloned.1.call-start = ((), (), s32[]{:S(2)}) async-start(), calls=%async_computation.8 | async-start | bytes 294912
  210.4 2.2 copy-start.2
  210.4 2.2 copy-start.5
  225.5 71.4 %copy-start.7 = (f32[1,64]{1,0:T(1,128)S(1)}, f32[1,64]{1,0:T(1,128)}, u32[]{:S(2)}) copy-start(f32[1,64]{1,0:T(1,128)} %param.9) | copy-start | bytes 772
Sparse Core Ops, SparseCore 0:
  146.3 64.0 all-reduce.1
  267.0 28.9 reduce-scatter.3

commit v2 on v1

v2 whole, which is shorter than its diff:
```python
import functools
import jax
import jax.numpy as jnp
from jax import lax
from jax.experimental import pallas as pl
from jax.experimental.pallas import tpu as pltpu
from jax.sharding import PartitionSpec as P

learning_rate = 0.2
Y = 4
MESH = pl.DeviceIdType.MESH


def kernel(
    n_wide, n_narrow,
    rows_ref, counts_ref, state_ref, down_ref, up_ref, bias_ref, grad_ref,
    crossed_ref, new_ref,
    raw, coded, ct, rows_all, pooled, passing, dense, down, up, bias, grad,
    rank_out, rank_in, ranks, cross_buf, grad_out, grad_pass, grad_in, row_out, row_in,
    load_sem, store_sem, send_sem, count_sem, row_sem, weight_sem, spread_sem, pass_sem,
    dense_sem, rank_sem, ranks_sem, back_sem, grad_sem, part_sem,
):
    f32, bf16 = jnp.float32, jnp.bfloat16
    Z, N = n_wide // Y, n_narrow
    half, pairs = Z // 2, N // 2
    block, cols = grad_ref.shape
    slots, rows_dev, emb = dense.shape[0], rows_ref.shape[1], rows_ref.shape[2]
    unit = Y * block
    w, n = lax.axis_index("wide"), lax.axis_index("narrow")
    z, y = w // Y, w % Y

    def shift(k, j):
        x, c = k // 2, k % 2
        if j == 0:
            near = jnp.where(x == 0, 0, half + x)
            return jnp.where(c == 0, half - x, near)
        return jnp.where(c == 0, 1 + x, Z - 1 - x)

    def unshift(d):
        j = jnp.where((d == 0) | ((d > pairs) & (d < Z - pairs)), 0, 1)
        c = jnp.where((d == 0) | (d > half), 1, 0)
        low = jnp.where(d > pairs, half - d, d - 1)
        high = jnp.where(d < Z - pairs, d - half, Z - 1 - d)
        x = jnp.where(d == 0, 0, jnp.where(d > half, high, low))
        return 2 * x + c, j

    pending = []

    def later(ref, i):
        pending.append(lambda: pltpu.make_async_copy(ref, ref, send_sem.at[i]).wait())

    def arrived(ref, sem):
        pltpu.make_async_copy(ref, ref, sem).wait()

    def remote(src, dst, i, sem, to):
        return pltpu.make_async_remote_copy(
            src_ref=src, dst_ref=dst, send_sem=send_sem.at[i], recv_sem=sem,
            device_id=to, device_id_type=MESH,
        )

    def finish():
        for wait in pending:
            wait()

    def load_unit(i, j):
        u = (z + shift((n + 1 + i) % N, j)) % Z
        pltpu.make_async_copy(
            counts_ref.at[0, :, pl.ds(pl.multiple_of(u * unit, unit), unit)], raw.at[u], load_sem.at[u]
        ).start()

    for j in range(2):
        pl.loop(0, N)(functools.partial(load_unit, j=j))
    first_col = pl.multiple_of(n * cols, cols)
    fixed = [
        pltpu.make_async_copy(bias_ref.at[:, pl.ds(first_col, cols)], bias, load_sem.at[Z]),
        pltpu.make_async_copy(grad_ref, grad, load_sem.at[Z + 1]),
        pltpu.make_async_copy(
            down_ref.at[pl.ds(pl.multiple_of(y * 16, 16), 16), pl.ds(first_col, cols)],
            down.at[y, n], load_sem.at[Z + 2]),
        pltpu.make_async_copy(
            up_ref.at[pl.ds(pl.multiple_of(z % Y * 16, 16), 16), pl.ds(first_col, cols)],
            up.at[z % Y, n], load_sem.at[Z + 3]),
    ]
    for copy in fixed:
        copy.start()

    barrier = pltpu.get_barrier_semaphore()

    @pl.loop(1, Y * N)
    def _(i):
        to = (y * N + n + i) % (Y * N)
        pl.semaphore_signal(barrier, inc=1, device_id=(z * Y + to // N, to % N), device_id_type=MESH)

    @pl.loop(1, Z)
    def _(i):
        pl.semaphore_signal(barrier, inc=1, device_id=((z + i) % Z * Y + y, n), device_id_type=MESH)

    def code_unit(i, j):
        u = (z + shift((n + 1 + i) % N, j)) % Z
        pltpu.make_async_copy(raw.at[u], raw.at[u], load_sem.at[u]).wait()
        coded[u] = raw[u].astype(f32).astype(bf16)

    pl.loop(0, N)(functools.partial(code_unit, j=0))
    rows_all[n] = rows_ref[0]
    pl.semaphore_wait(barrier, Y * N + Z - 2)

    @pl.loop(1, N)
    def _(i):
        k = (n + i) % N
        to_col = pl.multiple_of(k * cols, cols)
        remote(rows_ref.at[0], rows_all.at[n], 0, row_sem, (w, k)).start()
        remote(
            down_ref.at[pl.ds(pl.multiple_of(y * 16, 16), 16), pl.ds(to_col, cols)],
            down.at[y, n], 1, weight_sem.at[0], (w, k)).start()
        remote(
            up_ref.at[pl.ds(pl.multiple_of(z % Y * 16, 16), 16), pl.ds(to_col, cols)],
            up.at[z % Y, n], 2, weight_sem.at[1], (w, k)).start()

    def send_unit(i, j):
        k = (n + i) % N
        u = (z + shift(k, j)) % Z
        remote(coded.at[u], ct.at[j, n], 3 + j, count_sem.at[j], (w, k)).start()

    pl.loop(1, N)(functools.partial(send_unit, j=0))
    pl.loop(0, N)(functools.partial(code_unit, j=1))
    pl.loop(1, N)(functools.partial(send_unit, j=1))
    for j in range(2):
        ct[j, n] = coded[(z + shift(n, j)) % Z]
    later(rows_all.at[pl.ds(0, N - 1)], 0)
    later(down.at[0, pl.ds(0, N - 1)], 1)
    later(up.at[0, pl.ds(0, N - 1)], 2)
    for j in range(2):
        later(ct.at[j, pl.ds(0, N - 1)], 3 + j)

    for copy in fixed:
        copy.wait()
    arrived(down.at[y, pl.ds(0, N - 1)], weight_sem.at[0])
    for i in range(1, Y):
        remote(down.at[y], down.at[y], 5, spread_sem.at[0], (z * Y + (y + i) % Y, n)).start()
    later(down.at[pl.ds(0, Y - 1)], 5)
    arrived(up.at[z % Y, pl.ds(0, N - 1)], weight_sem.at[1])
    zq = z % Y
    for step in (1, Z - 1):
        remote(up.at[zq], up.at[zq], 6, spread_sem.at[1], ((z + step) % Z * Y + y, n)).start()
    for step, start in ((2, 0), (Z - 2, pairs)):
        part = up.at[zq, pl.ds(start, pairs)]
        remote(part, part, 6, spread_sem.at[1], ((z + step) % Z * Y + y, n)).start()
    later(up.at[pl.ds(0, Y - 1)], 6)

    arrived(rows_all.at[pl.ds(0, N - 1)], row_sem)
    table_rows = rows_all[...].reshape(N * rows_dev, emb)

    def along_z(src, dst, i, sem, far, to):
        @pl.when(far != 0)
        def _():
            remote(src, dst, i, sem, to).start()

        @pl.when(far == 0)
        def _():
            pltpu.make_async_copy(src, dst, sem).start()

        def wait():
            @pl.when(far != 0)
            def _():
                pltpu.make_async_copy(src, src, send_sem.at[i]).wait()

        pending.append(wait)

    def over_plane(src, dst, i, sem, to_w, to_n):
        is_me = (to_w == w) & (to_n == n)

        @pl.when(jnp.logical_not(is_me))
        def _():
            remote(src, dst, i, sem, (to_w, to_n)).start()

        @pl.when(is_me)
        def _():
            pltpu.make_async_copy(src, dst, sem).start()

        def wait():
            @pl.when(jnp.logical_not(is_me))
            def _():
                pltpu.make_async_copy(src, src, send_sem.at[i]).wait()

        pending.append(wait)

    for j in range(2):
        arrived(ct.at[j, pl.ds(0, N - 1)], count_sem.at[j])
        counts = ct[j].reshape(N * rows_dev, unit)
        pooled[j] = lax.dot_general(
            counts, table_rows, (((0,), (0,)), ((), ())), preferred_element_type=f32
        ).astype(bf16)
        far = shift(n, j)
        along_z(pooled.at[j], passing.at[j], 7 + j, pass_sem.at[j], far, ((z + far) % Z * Y + y, n))
    for j in range(2):
        arrived(passing.at[j], pass_sem.at[j])
        zt = (z + Z - shift(n, j)) % Z
        for i in range(Y):
            yd = (y + i) % Y
            over_plane(
                passing.at[j, pl.ds(pl.multiple_of(yd * block, 16), block)],
                dense.at[zt % 2 * Y + y], 9 + j * Y + i, dense_sem, z * Y + yd, zt // 2)

    arrived(down.at[pl.ds(0, Y - 1)], spread_sem.at[0])
    arrived(up.at[pl.ds(0, Y - 1)], spread_sem.at[1])
    arrived(dense, dense_sem)
    ranks_all = Y * N * 16
    dense_in = jnp.concatenate([dense[s] for s in range(slots)], axis=1)
    scaled = (grad[...].astype(f32) * dense_in.astype(f32)).astype(bf16)
    contract_cols = (((1,), (1,)), ((), ()))
    low = lax.dot_general(
        dense_in, down[...].reshape(ranks_all, cols), contract_cols, preferred_element_type=f32)
    rank_grad = lax.dot_general(
        scaled, up[...].reshape(ranks_all, cols), contract_cols, preferred_element_type=f32)
    for r in range(N // 2):
        rank_out[r] = low[:, r * emb:(r + 1) * emb].astype(bf16)
        rank_out[r + N // 2] = rank_grad[:, r * emb:(r + 1) * emb].astype(bf16)

    @pl.loop(1, N)
    def _(i):
        k = (n + i) % N
        remote(rank_out.at[k], rank_in.at[n], 17, rank_sem, (w, k)).start()

    later(rank_out.at[pl.ds(0, N - 1)], 17)
    rank_in[n] = rank_out[n]
    arrived(rank_in.at[pl.ds(0, N - 1)], rank_sem)
    ranks[n] = jnp.sum(rank_in[...].astype(f32), axis=0).astype(bf16)

    @pl.loop(1, N)
    def _(i):
        remote(ranks.at[n], ranks.at[n], 18, ranks_sem, (w, (n + i) % N)).start()

    later(ranks.at[pl.ds(0, N - 1)], 18)
    arrived(ranks.at[pl.ds(0, N - 1)], ranks_sem)
    low = jnp.concatenate([ranks[r] for r in range(N // 2)], axis=1)
    rank_grad = jnp.concatenate([ranks[r + N // 2] for r in range(N // 2)], axis=1)
    for s in range(slots):
        here = slice(s * emb, (s + 1) * emb)
        lifted = jnp.dot(
            low, down_cols(up, here, ranks_all), preferred_element_type=f32) + bias[:, here]
        back = jnp.dot(rank_grad, down_cols(down, here, ranks_all), preferred_element_type=f32)
        x = dense[s].astype(f32)
        grad_out[s] = (grad[:, here].astype(f32) * (lifted + 1.0) + back).astype(bf16)
        cross_buf[:, here] = (x * lifted + x).astype(bf16)
        zb, yt = s // Y, s % Y
        k, j = unshift((z + Z - (2 * n + zb)) % Z)
        over_plane(
            grad_out.at[s], grad_pass.at[j, pl.ds(pl.multiple_of(y * block, 16), block)],
            19 + s, back_sem.at[j], z * Y + yt, k)
    store = pltpu.make_async_copy(cross_buf, crossed_ref, store_sem)
    store.start()
    pending.append(store.wait)

    for j in range(2):
        arrived(grad_pass.at[j], back_sem.at[j])
        far = shift(n, j)
        along_z(
            grad_pass.at[j], grad_in.at[j], 27 + j, grad_sem.at[j], far,
            ((z + Z - far) % Z * Y + y, n))
    arrived(grad_in.at[0], grad_sem.at[0])
    part = jnp.dot(
        ct[0].reshape(N * rows_dev, unit), grad_in[0], preferred_element_type=f32)
    arrived(grad_in.at[1], grad_sem.at[1])
    part += jnp.dot(
        ct[1].reshape(N * rows_dev, unit), grad_in[1], preferred_element_type=f32)
    row_out[...] = part.reshape(N, rows_dev, emb)

    @pl.loop(1, N)
    def _(i):
        k = (n + i) % N
        remote(row_out.at[k], row_in.at[n], 29, part_sem, (w, k)).start()

    later(row_out.at[pl.ds(0, N - 1)], 29)
    row_in[n] = row_out[n]
    arrived(row_in.at[pl.ds(0, N - 1)], part_sem)
    row_grad = jnp.sum(row_in[...], axis=0)
    square = (rows_dev, rows_dev)
    diagonal = lax.broadcasted_iota(jnp.int32, square, 0) == lax.broadcasted_iota(jnp.int32, square, 1)
    state = jnp.sum(jnp.where(diagonal, state_ref[...], 0.0), axis=1, keepdims=True)
    state = state + jnp.mean(row_grad * row_grad, axis=1, keepdims=True)
    new_ref[0] = rows_ref[0].astype(f32) - learning_rate * row_grad / jnp.sqrt(state)
    finish()


def down_cols(ref, here, ranks_all):
    return ref[:, :, :, here].reshape(ranks_all, here.stop - here.start)


def on_device(gathered_rows, bag_counts, row_state, cross_down, cross_up, cross_bias, upstream):
    f32, bf16 = jnp.float32, jnp.bfloat16
    n_wide, n_narrow = lax.axis_size("wide"), lax.axis_size("narrow")
    Z, N = n_wide // Y, n_narrow
    rows_dev, emb = gathered_rows.shape[1:]
    block, cols = upstream.shape
    unit, slots = Y * block, cols // emb
    vmem = pl.BlockSpec(memory_space=pltpu.VMEM)
    hbm = pl.BlockSpec(memory_space=pl.ANY)
    dma = pltpu.SemaphoreType.DMA
    return pl.pallas_call(
        functools.partial(kernel, n_wide, n_narrow),
        out_shape=(
            jax.ShapeDtypeStruct((block, cols), bf16),
            jax.ShapeDtypeStruct((1, rows_dev, emb), f32),
        ),
        in_specs=[vmem, hbm, vmem, hbm, hbm, hbm, hbm],
        out_specs=(hbm, vmem),
        scratch_shapes=[
            pltpu.VMEM((Z, rows_dev, unit), jnp.int32),
            pltpu.VMEM((Z, rows_dev, unit), bf16),
            pltpu.VMEM((2, N, rows_dev, unit), bf16),
            pltpu.VMEM((N, rows_dev, emb), bf16),
            pltpu.VMEM((2, unit, emb), bf16),
            pltpu.VMEM((2, unit, emb), bf16),
            pltpu.VMEM((slots, block, emb), bf16),
            pltpu.VMEM((Y, N, 16, cols), bf16),
            pltpu.VMEM((Y, N, 16, cols), bf16),
            pltpu.VMEM((1, cols), f32),
            pltpu.VMEM((block, cols), bf16),
            pltpu.VMEM((N, block, emb), bf16),
            pltpu.VMEM((N, block, emb), bf16),
            pltpu.VMEM((N, block, emb), bf16),
            pltpu.VMEM((block, cols), bf16),
            pltpu.VMEM((slots, block, emb), bf16),
            pltpu.VMEM((2, unit, emb), bf16),
            pltpu.VMEM((2, unit, emb), bf16),
            pltpu.VMEM((N, rows_dev, emb), f32),
            pltpu.VMEM((N, rows_dev, emb), f32),
            dma((Z + 4,)), dma, dma((30,)), dma((2,)), dma, dma((2,)), dma((2,)), dma((2,)),
            dma, dma, dma, dma((2,)), dma((2,)), dma,
        ],
        compiler_params=pltpu.CompilerParams(
            collective_id=0, has_side_effects=True, vmem_limit_bytes=40 * 1024 * 1024
        ),
    )(
        gathered_rows, bag_counts, row_state, cross_down, cross_up,
        cross_bias.reshape(1, -1), upstream,
    )


def solution(mesh):
    placed = (
        P("wide", "narrow", None),
        P("wide", "narrow", None),
        P("wide", "narrow"),
        P("narrow", None),
        P("narrow", None),
        P(),
        P("wide", "narrow"),
    )
    return jax.shard_map(
        on_device,
        mesh=mesh,
        in_specs=placed,
        out_specs=(P("wide", "narrow"), P("wide", "narrow", None)),
        check_vma=False,
    )
```

time: 306 us -> 116 us (0.38)
  blocking collectives: 125 us -> 0 us
  waiting for transfers between devices: 113 us -> 0 us
  Pallas kernels: 0 us -> 105 us
  starting transfers between devices: 21.6 us -> 0 us
  local copies, waits for them, and re-layouts: 23.5 us -> 8.62 us
  between operations: 14.2 us -> 0.66 us
  matrix products: 4.65 us -> 0 us
    pallas_call x0 -> x1, Pallas kernels: none -> 105 us  [on_device(): pl.pallas_call(functools.partial(kernel, n_wide, n_narrow), out_shape=(ja...]
    all_to_all x3 -> x0, blocking collectives: 91.9 us -> none  [the longest x1 39.9 us: on_device(): lax.all_to_all(pooled.reshape(wide, sub, emb), 'wide', split_axis=0, conc...]
    psum x1 -> x0, waiting for transfers between devices: 63.5 us -> none  [on_device(): lax.psum(jnp.concatenate([low, rank_grad], axis=1).astype(bf16), 'narrow')]
    all_gather x1 -> x0, blocking collectives: 33 us -> none  [on_device(): rows_all = lax.all_gather(gathered_rows[0], 'narrow', axis=0, tiled=True)]
    unnamed x3 -> x0, waiting for transfers between devices: 29.1 us -> none
    all_to_all x3 -> x0, starting transfers between devices: 21.6 us -> none  [the longest x1 10.5 us: on_device(): lax.all_to_all(counts.reshape(n, rows_dev, wide * sub), 'narrow', split_a...]
    all_to_all x3 -> x0, waiting for transfers between devices: 20.2 us -> none  [the longest x1 13.8 us: on_device(): lax.all_to_all(counts.reshape(n, rows_dev, wide * sub), 'narrow', split_a...]
    convert_element_type x2 -> x0, local copies, waits for them, and re-layouts: 6.5 us -> none  [on_device(): bag_counts[0].astype(bf16).reshape(rows_dev, wide, n, sub)]
  transfers between devices with their start and end apart: 5 -> 0, of which waited for: 4 -> 0; matrix products, arithmetic and copies ran while one was open for 2% -> 0% of each run, Pallas kernels for 0% -> 0%
where the time goes in v2:
time: 116 us; the launch traced here: 115 us
  Pallas kernels  105 us (91%)
  local copies, waits for them, and re-layouts  8.62 us (7%)
    pallas_call x1, Pallas kernels, on_device(): pl.pallas_call(functools.partial(kernel, n_wide, n_narrow), out_shape=(ja...  105 us
    unnamed x16, local copies, waits for them, and re-layouts  8.62 us

profile of v2, /device:TPU:1, one launch (start us, length us, event | category | flops | bytes accessed | tf_op | source)
XLA Modules:
  0.0 114.7 jit_solution(5912290166478549607)
XLA Ops:
  0.6 0.0 copy-start
  0.6 1.7 %copy-done = s32[1,64,10240]{2,1,0:T(8,128)S(1)} copy-done((s32[1,64,10240]{2,1,0:T(8,128)S(1)}, s32[1,64,10240]{2,1,0:T(8,128)}, u32[]{:S(2)}) %copy-start) | copy-done | bytes 2621464
  2.4 0.0 copy-start.1
  2.4 1.2 %copy-done.1 = bf16[64,8192]{1,0:T(8,128)(2,1)S(1)} copy-done((bf16[64,8192]{1,0:T(8,128)(2,1)S(1)}, bf16[64,8192]{1,0:T(8,128)(2,1)}, u32[]{:S(2)}) %copy-start.1) | copy-done | bytes 1048600
  3.6 0.0 copy-start.2
  3.6 1.2 %copy-done.2 = bf16[64,8192]{1,0:T(8,128)(2,1)S(1)} copy-done((bf16[64,8192]{1,0:T(8,128)(2,1)S(1)}, bf16[64,8192]{1,0:T(8,128)(2,1)}, u32[]{:S(2)}) %copy-start.2) | copy-done | bytes 1048600
  4.8 0.0 copy-start.3
  4.8 1.0 copy-done.3
  5.8 0.0 copy-start.4
  5.8 0.8 copy-done.4
  6.6 0.0 copy-start.5
  6.6 0.7 copy-done.5
  7.3 0.0 copy-start.6
  7.3 0.7 copy-done.6
  7.9 105.4 %shard_map.86 = (bf16[160,1024]{1,0:T(8,128)(2,1)S(1)}, f32[1,64,128]{2,1,0:T(8,128)S(1)}) custom-call(bf16[1,64,128]{2,1,0:T(8,128)(2,1)S(1)} %copy-done.5, s32[1,64,10240]{2,1,0:T(8,128)S(1)} %copy-done, f32[1,64]{1,0:T(1,128)S(1)} %copy-done.6, bf16[64,8192]{1,0:T(8,128)(2,1)S(1)} %copy-done.1, bf16[64,8192]{1,0:T(8,128)(2,1)S(1)} %copy-done.2, ...), custom_call_target="tpu_custom_call" | custom-call | tf_op jit(solution)/shard_map/pallas_call | solution.py:299
  113.4 0.7 copy.11
  114.1 0.6 copy.12
Async XLA Ops:
  0.6 1.7 %copy-start = (s32[1,64,10240]{2,1,0:T(8,128)S(1)}, s32[1,64,10240]{2,1,0:T(8,128)}, u32[]{:S(2)}) copy-start(s32[1,64,10240]{2,1,0:T(8,128)} %counts_ref.1) | copy-start | bytes 7864324
  2.4 1.2 %copy-start.1 = (bf16[64,8192]{1,0:T(8,128)(2,1)S(1)}, bf16[64,8192]{1,0:T(8,128)(2,1)}, u32[]{:S(2)}) copy-start(bf16[64,8192]{1,0:T(8,128)(2,1)} %down_ref.1) | copy-start | bytes 3145732
  3.6 1.2 %copy-start.2 = (bf16[64,8192]{1,0:T(8,128)(2,1)S(1)}, bf16[64,8192]{1,0:T(8,128)(2,1)}, u32[]{:S(2)}) copy-start(bf16[64,8192]{1,0:T(8,128)(2,1)} %up_ref.1) | copy-start | bytes 3145732
  4.8 1.0 copy-start.3
  5.8 0.8 copy-start.4
  6.6 0.7 copy-start.5
  7.3 0.7 copy-start.6

commit v3 on v1

v3 whole, which is shorter than its diff:
```python
import functools
import types
import jax
import jax.numpy as jnp
from jax import lax
from jax.experimental import pallas as pl
from jax.experimental.pallas import tpu as pltpu
from jax.sharding import PartitionSpec as P

learning_rate = 0.2
Y = 4
RANK_ROWS = 16
MESH = pl.DeviceIdType.MESH


def split(block):
    first = -(-block // 64) * 32
    return first, block - first


def kernel(n_wide, n_narrow, names, *refs):
    m = types.SimpleNamespace(**dict(zip(names, refs, strict=True)))
    f32, bf16 = jnp.float32, jnp.bfloat16
    Z, N = n_wide // Y, n_narrow
    half, quarter = Z // 2, Z // 4
    block, cols = m.grad_ref.shape
    rows_dev, emb = m.rows_ref.shape[1:]
    slots = cols // emb
    unit, quad = Y * block, cols // Y
    per_quad = quad // emb
    ranks_all = Y * N * RANK_ROWS
    sizes = split(block)
    starts = (0, sizes[0])
    parts = range(2)
    w, n = lax.axis_index("wide"), lax.axis_index("narrow")
    z, y = w // Y, w % Y
    zq = z % Y

    def shift(k, j):
        x, c = k // 2, k % 2
        if j == 0:
            return jnp.where(c == 0, half - x, jnp.where(x == 0, Z - quarter, half + x))
        return jnp.where(
            c == 0, jnp.where(x == 0, quarter, x), jnp.where(x == 0, 0, Z - x))

    def unshift(d):
        e = jnp.where(d > half, Z - d, d)
        x = jnp.where(e == quarter, 0, jnp.where(e < quarter, e, half - e))
        c = jnp.where((d == 0) | (d > half), 1, 0)
        j = jnp.where((e > quarter) | (d == Z - quarter), 0, 1)
        return 2 * x + c, j

    pending = []
    used = [0]

    def new_send():
        used[0] += 1
        return m.send_sem.at[used[0] - 1]

    def wait_bytes(ref, sem):
        pltpu.make_async_copy(ref, ref, sem).wait()

    def later(ref, sem):
        pending.append(lambda: wait_bytes(ref, sem))

    def remote(src, dst, send, sem, to):
        return pltpu.make_async_remote_copy(
            src_ref=src, dst_ref=dst, send_sem=send, recv_sem=sem,
            device_id=to, device_id_type=MESH,
        )

    def move(src, dst, sem, here, to):
        send = new_send()

        @pl.when(jnp.logical_not(here))
        def _():
            remote(src, dst, send, sem, to).start()

        @pl.when(here)
        def _():
            pltpu.make_async_copy(src, dst, sem).start()

        def wait():
            @pl.when(jnp.logical_not(here))
            def _():
                wait_bytes(src, send)

        pending.append(wait)

    def finish():
        for wait in pending:
            wait()
        pending.clear()

    def load_unit(i, j):
        u = (z + shift((n + 1 + i) % N, j)) % Z
        pltpu.make_async_copy(
            m.counts_ref.at[0, :, pl.ds(pl.multiple_of(u * unit, unit), unit)],
            m.raw.at[u], m.load_sem.at[u],
        ).start()

    def chip_blocks(k):
        for which, ref in enumerate((m.down_ref, m.up_ref)):
            for q in range(Y):
                yield (
                    ref.at[:, :, pl.ds(pl.multiple_of(k * cols + q * quad, quad), quad)],
                    m.weights.at[which, q, :, n])

    pl.loop(0, N)(functools.partial(load_unit, j=0))
    fixed = [pltpu.make_async_copy(a, b, m.load_sem.at[Z + 2]) for a, b in chip_blocks(n)]
    own_blocks = m.weights.at[:, :, :, 0]

    def load_shares(k):
        for which, ref in enumerate((m.down_ref, m.up_ref)):
            pltpu.make_async_copy(
                ref.at[y, :, pl.ds(pl.multiple_of(k * cols + zq * quad, quad), quad)],
                m.shares.at[which, k], m.load_sem.at[Z + 3],
            ).start()

    small = [
        pltpu.make_async_copy(
            m.bias_ref.at[:, pl.ds(pl.multiple_of(n * cols, cols), cols)],
            m.bias, m.load_sem.at[Z]),
        pltpu.make_async_copy(m.grad_ref, m.grad, m.load_sem.at[Z + 1]),
    ]
    pl.loop(0, N)(load_shares)
    pl.loop(0, N)(functools.partial(load_unit, j=1))
    for copy in small + fixed:
        copy.start()

    barrier = pltpu.get_barrier_semaphore()

    @pl.loop(1, Y * N)
    def _(i):
        to = (y * N + n + i) % (Y * N)
        pl.semaphore_signal(barrier, inc=1, device_id=(z * Y + to // N, to % N), device_id_type=MESH)

    @pl.loop(1, Z)
    def _(i):
        pl.semaphore_signal(barrier, inc=1, device_id=((z + i) % Z * Y + y, n), device_id_type=MESH)

    @pl.loop(0, slots)
    def _(i):
        zt, yt = 2 * n + i // Y, i % Y
        k, _ = unshift((z + Z - zt) % Z)

        @pl.when(jnp.logical_not((zt == z) & (yt == y) & (k == n)))
        def _():
            pl.semaphore_signal(barrier, inc=1, device_id=(zt * Y + yt, k), device_id_type=MESH)

    pools_for_itself = jnp.where((shift(n, 1) == 0) & (z // 2 == n), 1, 0)

    def code_unit(i, j):
        u = (z + shift((n + 1 + i) % N, j)) % Z
        wait_bytes(m.raw.at[u], m.load_sem.at[u])
        values = m.raw[u].astype(f32)
        for h in parts:
            lanes = [
                values[:, a * block + starts[h]:a * block + starts[h] + sizes[h]] for a in range(Y)]
            m.coded[h][u] = jnp.concatenate(lanes, axis=1).astype(bf16)

    pl.loop(0, N)(functools.partial(code_unit, j=0))
    m.rows_all[n] = m.rows_ref[0]
    wait_bytes(m.shares, m.load_sem.at[Z + 3])
    pl.semaphore_wait(barrier, Y * N + Z - 2 + slots - pools_for_itself)

    sends = [new_send() for _ in range(3)]

    @pl.loop(2, N)
    def _(i):
        k = (n // 2 * 2 + i) % N
        remote(m.shares.at[:, k], m.weights.at[:, zq, y, n], sends[1], m.column_sem.at[0], (w, k)).start()

    @pl.loop(1, N)
    def _(i):
        remote(m.rows_ref.at[0], m.rows_all.at[n], sends[0], m.row_sem, (w, (n + i) % N)).start()

    later(m.rows_all.at[pl.ds(0, N - 1)], sends[0])
    later(m.weights.at[:, 0, 0, pl.ds(0, N - 2)], sends[1])

    def to_sibling():
        sibling = (w, n + 1 - 2 * (n % 2))
        for a, b in chip_blocks(sibling[1]):
            remote(a, b, sends[2], m.sibling_sem, sibling).start()
        later(own_blocks, sends[2])

    others = [pl.ds((n // 2 + i) % (N // 2) * 2, 2) for i in range(1, N // 2)]

    def spread_columns():
        wait_bytes(m.weights.at[:, 0, 0, pl.ds(0, N - 2)], m.column_sem.at[0])
        send = new_send()
        for step in (1, Z - 1, 2, Z - 2):
            for ds in others:
                part = m.weights.at[:, zq, y, ds]
                if step in (2, Z - 2):
                    part = m.weights.at[0 if step == 2 else 1, zq, y, ds]
                remote(part, part, send, m.column_sem.at[1], ((z + step) % Z * Y + y, n)).start()
        later(m.weights.at[:, pl.ds(0, Y - 1), 0, pl.ds(0, N - 2)], send)

    def spread_ranks():
        wait_bytes(m.weights.at[:, pl.ds(0, Y - 1), 0, pl.ds(0, N - 2)], m.column_sem.at[1])
        for which in range(2):
            send = new_send()
            for step in (1, Y - 1):
                for ds in others:
                    part = m.weights.at[which, :, y, ds]
                    remote(
                        part, part, send, m.rank_block_sem.at[which, 0], (z * Y + (y + step) % Y, n)
                    ).start()
            later(m.weights.at[which, :, pl.ds(0, 2), pl.ds(0, N - 2)], send)

    def forward_ranks(which):
        wait_bytes(m.weights.at[which, :, pl.ds(0, 2), pl.ds(0, N - 2)], m.rank_block_sem.at[which, 0])
        send = new_send()
        for step, start in ((1, 0), (Y - 1, Y // 2)):
            for ds in others:
                part = m.weights.at[which, pl.ds(start, Y // 2), (y + Y - step) % Y, ds]
                remote(
                    part, part, send, m.rank_block_sem.at[which, 1], (z * Y + (y + step) % Y, n)
                ).start()
        later(m.weights.at[which, :, 0, pl.ds(0, N - 2)], send)

    def weights_here(which):
        wait_bytes(m.weights.at[which, :, 0, pl.ds(0, N - 2)], m.rank_block_sem.at[which, 1])

    def small_here():
        wait_bytes(own_blocks, m.sibling_sem)
        for copy in small + fixed:
            copy.wait()

    def send_units(h, j):
        send = new_send()

        @pl.loop(1, N)
        def _(i):
            k = (n + i) % N
            u = (z + shift(k, j)) % Z
            remote(m.coded[h].at[u], m.ct[h].at[j, n], send, m.count_sem.at[h, j], (w, k)).start()

        later(m.ct[h].at[j, pl.ds(0, N - 1)], send)

    spread_columns()
    send_units(0, 0)
    pl.loop(0, N)(functools.partial(code_unit, j=1))
    send_units(0, 1)
    to_sibling()
    spread_ranks()
    send_units(1, 0)
    send_units(1, 1)
    for h in parts:
        for j in range(2):
            m.ct[h][j, n] = m.coded[h][(z + shift(n, j)) % Z]

    def pool(h, j):
        wait_bytes(m.ct[h].at[j, pl.ds(0, N - 1)], m.count_sem.at[h, j])
        counts = m.ct[h][j].reshape(N * rows_dev, Y * sizes[h])
        table_rows = m.rows_all[...].reshape(N * rows_dev, emb)
        m.pooled[h][j] = lax.dot_general(
            counts, table_rows, (((0,), (0,)), ((), ())), preferred_element_type=f32
        ).astype(bf16)
        far = shift(n, j)
        zw = (z + far) % Z
        size = sizes[h]
        for i in range(Y):
            yd = (y + i) % Y
            move(
                m.pooled[h].at[j, pl.ds(pl.multiple_of(yd * size, 16), size)],
                m.dense[h].at[z % 2 * Y + y], m.dense_sem.at[h],
                (yd == y) & (z // 2 == n) & (zw == z), (zw * Y + yd, z // 2))

    def to_ranks(h):
        wait_bytes(m.dense[h], m.dense_sem.at[h])
        rows = pl.ds(starts[h], sizes[h])
        width = ranks_all * 2 // N
        send = new_send()
        for which in range(2):
            if h == 0:
                weights_here(which)
            total = 0.0
            for q in range(Y):
                x = jnp.concatenate(
                    [m.dense[h][q * per_quad + s] for s in range(per_quad)], axis=1)
                if which == 1:
                    slope = m.grad[rows, q * quad:(q + 1) * quad].astype(f32)
                    x = (slope * x.astype(f32)).astype(bf16)
                total += lax.dot_general(
                    x, m.weights[which, q].reshape(ranks_all, quad), (((1,), (1,)), ((), ())),
                    preferred_element_type=f32)
            first = which * (N // 2)
            for r in range(N // 2):
                m.rank_out[h][first + r] = total[:, r * width:(r + 1) * width].astype(bf16)

            @pl.loop(0, N // 2)
            def _(i):
                k = first + (n + i) % (N // 2)

                @pl.when(k != n)
                def _():
                    remote(
                        m.rank_out[h].at[k], m.rank_in[h].at[n], send, m.rank_sem.at[h], (w, k)
                    ).start()

        later(m.rank_out[h].at[pl.ds(0, N - 1)], send)
        m.rank_in[h][n] = m.rank_out[h][n]

    def sum_ranks(h):
        wait_bytes(m.rank_in[h].at[pl.ds(0, N - 1)], m.rank_sem.at[h])
        m.ranks[h][n] = jnp.sum(m.rank_in[h][...].astype(f32), axis=0).astype(bf16)
        send = new_send()

        @pl.loop(1, N)
        def _(i):
            remote(
                m.ranks[h].at[n], m.ranks[h].at[n], send, m.ranks_sem.at[h], (w, (n + i) % N)
            ).start()

        later(m.ranks[h].at[pl.ds(0, N - 1)], send)

    def from_ranks(h):
        wait_bytes(m.ranks[h].at[pl.ds(0, N - 1)], m.ranks_sem.at[h])
        size = sizes[h]
        rows = pl.ds(starts[h], size)
        low = jnp.concatenate([m.ranks[h][r] for r in range(N // 2)], axis=1)
        rank_grad = jnp.concatenate([m.ranks[h][r] for r in range(N // 2, N)], axis=1)
        for q in range(Y):
            here = slice(q * quad, (q + 1) * quad)
            lifted = jnp.dot(
                low, m.weights[1, q].reshape(ranks_all, quad), preferred_element_type=f32) + m.bias[:, here]
            back = jnp.dot(
                rank_grad, m.weights[0, q].reshape(ranks_all, quad), preferred_element_type=f32)
            x = jnp.concatenate(
                [m.dense[h][q * per_quad + s] for s in range(per_quad)], axis=1).astype(f32)
            slope = (m.grad[rows, here].astype(f32) * (lifted + 1.0) + back).astype(bf16)
            m.cross_buf[rows, here] = (x * lifted + x).astype(bf16)
            for s in range(per_quad):
                slot = q * per_quad + s
                m.grad_out[h][slot] = slope[:, s * emb:(s + 1) * emb]
                k, j = unshift((z + Z - (2 * n + slot // Y)) % Z)
                yt = slot % Y
                move(
                    m.grad_out[h].at[slot],
                    m.grad_pass[h].at[j, pl.ds(pl.multiple_of(y * size, 16), size)],
                    m.back_sem.at[h, j], (yt == y) & (k == n), (z * Y + yt, k))
        store = pltpu.make_async_copy(m.cross_buf.at[rows], m.crossed_ref.at[rows], m.store_sem.at[h])
        store.start()
        pending.append(store.wait)

    def pass_back(h, j):
        wait_bytes(m.grad_pass[h].at[j], m.back_sem.at[h, j])
        far = shift(n, j)
        move(
            m.grad_pass[h].at[j], m.grad_in[h].at[j], m.grad_sem.at[h, j],
            far == 0, ((z + Z - far) % Z * Y + y, n))

    def row_part(h, j):
        wait_bytes(m.grad_in[h].at[j], m.grad_sem.at[h, j])
        return jnp.dot(
            m.ct[h][j].reshape(N * rows_dev, Y * sizes[h]), m.grad_in[h][j],
            preferred_element_type=f32)

    wait_bytes(m.rows_all.at[pl.ds(0, N - 1)], m.row_sem)
    pool(0, 0)
    pool(0, 1)
    forward_ranks(0)
    pool(1, 0)
    forward_ranks(1)
    pool(1, 1)
    small_here()
    to_ranks(0)
    sum_ranks(0)
    to_ranks(1)
    from_ranks(0)
    sum_ranks(1)
    pass_back(0, 0)
    pass_back(0, 1)
    from_ranks(1)
    pass_back(1, 0)
    pass_back(1, 1)
    part = row_part(0, 0) + row_part(0, 1)
    part += row_part(1, 0)
    part += row_part(1, 1)
    m.row_out[...] = part.astype(bf16).reshape(N, rows_dev, emb)
    last = new_send()

    @pl.loop(1, N)
    def _(i):
        k = (n + i) % N
        remote(m.row_out.at[k], m.row_in.at[n], last, m.part_sem, (w, k)).start()

    m.row_in[n] = m.row_out[n]
    square = (rows_dev, rows_dev)
    diagonal = lax.broadcasted_iota(jnp.int32, square, 0) == lax.broadcasted_iota(jnp.int32, square, 1)
    state = jnp.sum(jnp.where(diagonal, m.state_ref[...], 0.0), axis=1, keepdims=True)
    finish()
    wait_bytes(m.row_in.at[pl.ds(0, N - 1)], m.part_sem)
    row_grad = jnp.sum(m.row_in[...].astype(f32), axis=0)
    state = state + jnp.mean(row_grad * row_grad, axis=1, keepdims=True)
    m.new_ref[0] = m.rows_ref[0].astype(f32) - learning_rate * row_grad / jnp.sqrt(state)
    wait_bytes(m.row_out.at[pl.ds(0, N - 1)], last)


def on_device(gathered_rows, bag_counts, row_state, cross_down, cross_up, cross_bias, upstream):
    f32, bf16 = jnp.float32, jnp.bfloat16
    n_wide, N = lax.axis_size("wide"), lax.axis_size("narrow")
    Z = n_wide // Y
    rows_dev, emb = gathered_rows.shape[1:]
    block, cols = upstream.shape
    unit, slots = Y * block, cols // emb
    width = 2 * cross_down.shape[0]
    sizes = split(block)
    vmem = pl.BlockSpec(memory_space=pltpu.VMEM)
    hbm = pl.BlockSpec(memory_space=pl.ANY)
    dma = pltpu.SemaphoreType.DMA

    def both(shape_of, dtype=bf16):
        return tuple(pltpu.VMEM(shape_of(size), dtype) for size in sizes)

    scratch = dict(
        raw=pltpu.VMEM((Z, rows_dev, unit), jnp.int32),
        coded=both(lambda size: (Z, rows_dev, Y * size)),
        ct=both(lambda size: (2, N, rows_dev, Y * size)),
        rows_all=pltpu.VMEM((N, rows_dev, emb), bf16),
        pooled=both(lambda size: (2, Y * size, emb)),
        dense=both(lambda size: (slots, size, emb)),
        weights=pltpu.VMEM((2, Y, Y, N, RANK_ROWS, cols // Y), bf16),
        shares=pltpu.VMEM((2, N, RANK_ROWS, cols // Y), bf16),
        bias=pltpu.VMEM((1, cols), f32),
        grad=pltpu.VMEM((block, cols), bf16),
        rank_out=both(lambda size: (N, size, width)),
        rank_in=both(lambda size: (N, size, width)),
        ranks=both(lambda size: (N, size, width)),
        cross_buf=pltpu.VMEM((block, cols), bf16),
        grad_out=both(lambda size: (slots, size, emb)),
        grad_pass=both(lambda size: (2, Y * size, emb)),
        grad_in=both(lambda size: (2, Y * size, emb)),
        row_out=pltpu.VMEM((N, rows_dev, emb), bf16),
        row_in=pltpu.VMEM((N, rows_dev, emb), bf16),
        load_sem=dma((Z + 4,)), store_sem=dma((2,)), send_sem=dma((64,)),
        count_sem=dma((2, 2)), row_sem=dma, column_sem=dma((2,)), rank_block_sem=dma((2, 2)),
        dense_sem=dma((2,)), rank_sem=dma((2,)), ranks_sem=dma((2,)),
        back_sem=dma((2, 2)), grad_sem=dma((2, 2)), part_sem=dma, sibling_sem=dma,
    )
    names = (
        "rows_ref", "counts_ref", "state_ref", "down_ref", "up_ref", "bias_ref", "grad_ref",
        "crossed_ref", "new_ref", *scratch)
    return pl.pallas_call(
        functools.partial(kernel, n_wide, N, names),
        out_shape=(
            jax.ShapeDtypeStruct((block, cols), bf16),
            jax.ShapeDtypeStruct((1, rows_dev, emb), f32),
        ),
        in_specs=[vmem, hbm, vmem, hbm, hbm, hbm, hbm],
        out_specs=(hbm, vmem),
        scratch_shapes=tuple(scratch.values()),
        compiler_params=pltpu.CompilerParams(
            collective_id=0, has_side_effects=True, vmem_limit_bytes=60 * 1024 * 1024
        ),
    )(
        gathered_rows, bag_counts, row_state, cross_down.reshape(Y, RANK_ROWS, -1),
        cross_up.reshape(Y, RANK_ROWS, -1), cross_bias.reshape(1, -1), upstream,
    )


def solution(mesh):
    placed = (
        P("wide", "narrow", None),
        P("wide", "narrow", None),
        P("wide", "narrow"),
        P("narrow", None),
        P("narrow", None),
        P(),
        P("wide", "narrow"),
    )
    return jax.shard_map(
        on_device,
        mesh=mesh,
        in_specs=placed,
        out_specs=(P("wide", "narrow"), P("wide", "narrow", None)),
        check_vma=False,
    )
```

time: 306 us -> 91.3 us (0.30)
  blocking collectives: 125 us -> 0 us
  waiting for transfers between devices: 113 us -> 0 us
  Pallas kernels: 0 us -> 87.3 us
  starting transfers between devices: 21.6 us -> 0 us
  local copies, waits for them, and re-layouts: 23.5 us -> 3.09 us
  between operations: 14.2 us -> 0.64 us
  matrix products: 4.65 us -> 0 us
    all_to_all x3 -> x0, blocking collectives: 91.9 us -> none  [the longest x1 39.9 us: on_device(): lax.all_to_all(pooled.reshape(wide, sub, emb), 'wide', split_axis=0, conc...]
    pallas_call x0 -> x1, Pallas kernels: none -> 87.3 us  [on_device(): pl.pallas_call(functools.partial(kernel, n_wide, N, names), out_shape=(ja...]
    psum x1 -> x0, waiting for transfers between devices: 63.5 us -> none  [on_device(): lax.psum(jnp.concatenate([low, rank_grad], axis=1).astype(bf16), 'narrow')]
    all_gather x1 -> x0, blocking collectives: 33 us -> none  [on_device(): rows_all = lax.all_gather(gathered_rows[0], 'narrow', axis=0, tiled=True)]
    unnamed x3 -> x0, waiting for transfers between devices: 29.1 us -> none
    all_to_all x3 -> x0, starting transfers between devices: 21.6 us -> none  [the longest x1 10.5 us: on_device(): lax.all_to_all(counts.reshape(n, rows_dev, wide * sub), 'narrow', split_a...]
    all_to_all x3 -> x0, waiting for transfers between devices: 20.2 us -> none  [the longest x1 13.8 us: on_device(): lax.all_to_all(counts.reshape(n, rows_dev, wide * sub), 'narrow', split_a...]
    convert_element_type x2 -> x0, local copies, waits for them, and re-layouts: 6.5 us -> none  [on_device(): bag_counts[0].astype(bf16).reshape(rows_dev, wide, n, sub)]
  transfers between devices with their start and end apart: 5 -> 0, of which waited for: 4 -> 0; matrix products, arithmetic and copies ran while one was open for 2% -> 0% of each run, Pallas kernels for 0% -> 0%
where the time goes in v3:
time: 91.3 us; the launch traced here: 91 us
  Pallas kernels  87.3 us (96%)
  local copies, waits for them, and re-layouts  3.09 us (3%)
    pallas_call x1, Pallas kernels, on_device(): pl.pallas_call(functools.partial(kernel, n_wide, N, names), out_shape=(ja...  87.3 us
    unnamed x2, local copies, waits for them, and re-layouts  3.09 us

profile of v3, /device:TPU:1, one launch (start us, length us, event | category | flops | bytes accessed | tf_op | source)
XLA Modules:
  0.0 91.0 jit_solution(14538391974065020822)
XLA Ops:
  0.6 87.3 %shard_map.86 = (bf16[160,1024]{1,0:T(8,128)(2,1)}, f32[1,64,128]{2,1,0:T(8,128)}) custom-call(bf16[1,64,128]{2,1,0:T(8,128)(2,1)} %refs_0_.1, s32[1,64,10240]{2,1,0:T(8,128)} %refs_1_.1, f32[1,64]{1,0:T(1,128)} %refs_2_.1, bf16[4,16,8192]{2,1,0:T(8,128)(2,1)} %bitcast.3, bf16[4,16,8192]{2,1,0:T(8,128)(2,1)} %bitcast.4, f32[1,8192]{1,0:T(1,128)} %bitcast.5, ...), custom_call_target="tpu_custom_call" | custom-call | tf_op jit(solution)/shard_map/pallas_call | solution.py:446
  87.9 1.7 %copy.11 = bf16[160,1024]{1,0:T(8,128)(2,1)} copy(bf16[160,1024]{1,0:T(8,128)(2,1)} %get-tuple-element.4) | data formatting | bytes 655360
  89.7 1.4 %copy.12 = f32[1,64,128]{2,1,0:T(8,128)} copy(f32[1,64,128]{2,1,0:T(8,128)} %get-tuple-element.5) | data formatting | bytes 65536

commit v4 on v3

--- a/solution.py
+++ b/solution.py
@@ -14,8 +14,8 @@
 
 
 def split(block):
-    first = -(-block // 64) * 32
-    return first, block - first
+    most = -(-block // 96) * 32
+    return tuple(min(most, block - first) for first in range(0, block, most))
 
 
 def kernel(n_wide, n_narrow, names, *refs):
@@ -30,8 +30,8 @@
     per_quad = quad // emb
     ranks_all = Y * N * RANK_ROWS
     sizes = split(block)
-    starts = (0, sizes[0])
-    parts = range(2)
+    starts = [sum(sizes[:h]) for h in range(len(sizes))]
+    parts = range(len(sizes))
     w, n = lax.axis_index("wide"), lax.axis_index("narrow")
     z, y = w // Y, w % Y
     zq = z % Y
@@ -111,11 +111,14 @@
     own_blocks = m.weights.at[:, :, :, 0]
 
     def load_shares(k):
-        for which, ref in enumerate((m.down_ref, m.up_ref)):
+        def load(ref, q, into):
+            first = pl.multiple_of(k * cols + q * quad, quad)
             pltpu.make_async_copy(
-                ref.at[y, :, pl.ds(pl.multiple_of(k * cols + zq * quad, quad), quad)],
-                m.shares.at[which, k], m.load_sem.at[Z + 3],
-            ).start()
+                ref.at[y, :, pl.ds(first, quad)], into, m.load_sem.at[Z + 3]).start()
+
+        for q in range(Y):
+            load(m.down_ref, q, m.down_share.at[k, q])
+        load(m.up_ref, zq, m.up_share.at[k])
 
     small = [
         pltpu.make_async_copy(
@@ -135,9 +138,14 @@
         to = (y * N + n + i) % (Y * N)
         pl.semaphore_signal(barrier, inc=1, device_id=(z * Y + to // N, to % N), device_id_type=MESH)
 
-    @pl.loop(1, Z)
-    def _(i):
-        pl.semaphore_signal(barrier, inc=1, device_id=((z + i) % Z * Y + y, n), device_id_type=MESH)
+    for step in (1, 2, Z - 2, Z - 1):
+        pl.semaphore_signal(barrier, inc=1, device_id=((z + step) % Z * Y + y, n), device_id_type=MESH)
+
+    for j in range(2):
+        @pl.when(shift(n, j) != 0)
+        def _():
+            to = (z + shift(n, j)) % Z * Y + y
+            pl.semaphore_signal(barrier, inc=1, device_id=(to, n), device_id_type=MESH)
 
     @pl.loop(0, slots)
     def _(i):
@@ -161,22 +169,34 @@
 
     pl.loop(0, N)(functools.partial(code_unit, j=0))
     m.rows_all[n] = m.rows_ref[0]
-    wait_bytes(m.shares, m.load_sem.at[Z + 3])
-    pl.semaphore_wait(barrier, Y * N + Z - 2 + slots - pools_for_itself)
-
-    sends = [new_send() for _ in range(3)]
+    wait_bytes(m.down_share, m.load_sem.at[Z + 3])
+    wait_bytes(m.up_share, m.load_sem.at[Z + 3])
+    pl.semaphore_wait(
+        barrier, Y * N + 5 + slots - pools_for_itself - jnp.where(shift(n, 1) == 0, 1, 0))
+
+    sends = [new_send() for _ in range(4)]
 
     @pl.loop(2, N)
     def _(i):
         k = (n // 2 * 2 + i) % N
-        remote(m.shares.at[:, k], m.weights.at[:, zq, y, n], sends[1], m.column_sem.at[0], (w, k)).start()
+        remote(
+            m.down_share.at[k], m.weights.at[0, :, y, n], sends[1], m.column_sem.at[0], (w, k)
+        ).start()
+
+    @pl.loop(2, N)
+    def _(i):
+        k = (n // 2 * 2 + i) % N
+        remote(
+            m.up_share.at[k], m.weights.at[1, zq, y, n], sends[3], m.column_sem.at[2], (w, k)
+        ).start()
 
     @pl.loop(1, N)
     def _(i):
         remote(m.rows_ref.at[0], m.rows_all.at[n], sends[0], m.row_sem, (w, (n + i) % N)).start()
 
     later(m.rows_all.at[pl.ds(0, N - 1)], sends[0])
-    later(m.weights.at[:, 0, 0, pl.ds(0, N - 2)], sends[1])
+    later(m.weights.at[0, :, 0, pl.ds(0, N - 2)], sends[1])
+    later(m.weights.at[1, 0, 0, pl.ds(0, N - 2)], sends[3])
 
     def to_sibling():
         sibling = (w, n + 1 - 2 * (n % 2))
@@ -184,37 +204,39 @@
             remote(a, b, sends[2], m.sibling_sem, sibling).start()
         later(own_blocks, sends[2])
 
-    others = [pl.ds((n // 2 + i) % (N // 2) * 2, 2) for i in range(1, N // 2)]
+    others = [(n // 2 + i) % (N // 2) * 2 for i in range(1, N // 2)]
 
     def spread_columns():
-        wait_bytes(m.weights.at[:, 0, 0, pl.ds(0, N - 2)], m.column_sem.at[0])
+        wait_bytes(m.weights.at[1, 0, 0, pl.ds(0, N - 2)], m.column_sem.at[2])
         send = new_send()
         for step in (1, Z - 1, 2, Z - 2):
-            for ds in others:
-                part = m.weights.at[:, zq, y, ds]
+            for k in others:
+                part = m.weights.at[1, zq, y, pl.ds(k, 2)]
                 if step in (2, Z - 2):
-                    part = m.weights.at[0 if step == 2 else 1, zq, y, ds]
+                    part = m.weights.at[1, zq, y, k + (0 if step == 2 else 1)]
                 remote(part, part, send, m.column_sem.at[1], ((z + step) % Z * Y + y, n)).start()
-        later(m.weights.at[:, pl.ds(0, Y - 1), 0, pl.ds(0, N - 2)], send)
-
-    def spread_ranks():
-        wait_bytes(m.weights.at[:, pl.ds(0, Y - 1), 0, pl.ds(0, N - 2)], m.column_sem.at[1])
-        for which in range(2):
-            send = new_send()
-            for step in (1, Y - 1):
-                for ds in others:
-                    part = m.weights.at[which, :, y, ds]
-                    remote(
-                        part, part, send, m.rank_block_sem.at[which, 0], (z * Y + (y + step) % Y, n)
-                    ).start()
-            later(m.weights.at[which, :, pl.ds(0, 2), pl.ds(0, N - 2)], send)
+        later(m.weights.at[1, pl.ds(0, Y - 1), 0, pl.ds(0, N - 2)], send)
+
+    def spread_ranks(which):
+        if which == 0:
+            wait_bytes(m.weights.at[0, :, 0, pl.ds(0, N - 2)], m.column_sem.at[0])
+        else:
+            wait_bytes(m.weights.at[1, pl.ds(0, Y - 1), 0, pl.ds(0, N - 2)], m.column_sem.at[1])
+        send = new_send()
+        for step in (1, Y - 1):
+            for k in others:
+                part = m.weights.at[which, :, y, pl.ds(k, 2)]
+                remote(
+                    part, part, send, m.rank_block_sem.at[which, 0], (z * Y + (y + step) % Y, n)
+                ).start()
+        later(m.weights.at[which, :, pl.ds(0, 2), pl.ds(0, N - 2)], send)
 
     def forward_ranks(which):
         wait_bytes(m.weights.at[which, :, pl.ds(0, 2), pl.ds(0, N - 2)], m.rank_block_sem.at[which, 0])
         send = new_send()
         for step, start in ((1, 0), (Y - 1, Y // 2)):
-            for ds in others:
-                part = m.weights.at[which, pl.ds(start, Y // 2), (y + Y - step) % Y, ds]
+            for k in others:
+                part = m.weights.at[which, pl.ds(start, Y // 2), (y + Y - step) % Y, pl.ds(k, 2)]
                 remote(
                     part, part, send, m.rank_block_sem.at[which, 1], (z * Y + (y + step) % Y, n)
                 ).start()
@@ -239,14 +261,15 @@
 
         later(m.ct[h].at[j, pl.ds(0, N - 1)], send)
 
-    spread_columns()
     send_units(0, 0)
     pl.loop(0, N)(functools.partial(code_unit, j=1))
     send_units(0, 1)
+    spread_ranks(0)
+    spread_columns()
+    for h in parts[1:]:
+        send_units(h, 0)
+        send_units(h, 1)
     to_sibling()
-    spread_ranks()
-    send_units(1, 0)
-    send_units(1, 1)
     for h in parts:
         for j in range(2):
             m.ct[h][j, n] = m.coded[h][(z + shift(n, j)) % Z]
@@ -359,26 +382,34 @@
             preferred_element_type=f32)
 
     wait_bytes(m.rows_all.at[pl.ds(0, N - 1)], m.row_sem)
+    spread_ranks(1)
     pool(0, 0)
     pool(0, 1)
     forward_ranks(0)
     pool(1, 0)
     forward_ranks(1)
     pool(1, 1)
+    for h in parts[2:]:
+        pool(h, 0)
+        pool(h, 1)
     small_here()
+
+    def step_back(h):
+        pass_back(h, 0)
+        pass_back(h, 1)
+
     to_ranks(0)
-    sum_ranks(0)
-    to_ranks(1)
-    from_ranks(0)
-    sum_ranks(1)
-    pass_back(0, 0)
-    pass_back(0, 1)
-    from_ranks(1)
-    pass_back(1, 0)
-    pass_back(1, 1)
-    part = row_part(0, 0) + row_part(0, 1)
-    part += row_part(1, 0)
-    part += row_part(1, 1)
+    for h in parts:
+        sum_ranks(h)
+        if h + 1 < len(sizes):
+            to_ranks(h + 1)
+        if h > 0:
+            step_back(h - 1)
+        from_ranks(h)
+    step_back(parts[-1])
+    part = 0.0
+    for h in parts:
+        part += row_part(h, 0) + row_part(h, 1)
     m.row_out[...] = part.astype(bf16).reshape(N, rows_dev, emb)
     last = new_send()
 
@@ -408,37 +439,39 @@
     unit, slots = Y * block, cols // emb
     width = 2 * cross_down.shape[0]
     sizes = split(block)
+    n_parts = len(sizes)
     vmem = pl.BlockSpec(memory_space=pltpu.VMEM)
     hbm = pl.BlockSpec(memory_space=pl.ANY)
     dma = pltpu.SemaphoreType.DMA
 
-    def both(shape_of, dtype=bf16):
+    def each(shape_of, dtype=bf16):
         return tuple(pltpu.VMEM(shape_of(size), dtype) for size in sizes)
 
     scratch = dict(
         raw=pltpu.VMEM((Z, rows_dev, unit), jnp.int32),
-        coded=both(lambda size: (Z, rows_dev, Y * size)),
-        ct=both(lambda size: (2, N, rows_dev, Y * size)),
+        coded=each(lambda size: (Z, rows_dev, Y * size)),
+        ct=each(lambda size: (2, N, rows_dev, Y * size)),
         rows_all=pltpu.VMEM((N, rows_dev, emb), bf16),
-        pooled=both(lambda size: (2, Y * size, emb)),
-        dense=both(lambda size: (slots, size, emb)),
+        pooled=each(lambda size: (2, Y * size, emb)),
+        dense=each(lambda size: (slots, size, emb)),
         weights=pltpu.VMEM((2, Y, Y, N, RANK_ROWS, cols // Y), bf16),
-        shares=pltpu.VMEM((2, N, RANK_ROWS, cols // Y), bf16),
+        down_share=pltpu.VMEM((N, Y, RANK_ROWS, cols // Y), bf16),
+        up_share=pltpu.VMEM((N, RANK_ROWS, cols // Y), bf16),
         bias=pltpu.VMEM((1, cols), f32),
         grad=pltpu.VMEM((block, cols), bf16),
-        rank_out=both(lambda size: (N, size, width)),
-        rank_in=both(lambda size: (N, size, width)),
-        ranks=both(lambda size: (N, size, width)),
+        rank_out=each(lambda size: (N, size, width)),
+        rank_in=each(lambda size: (N, size, width)),
+        ranks=each(lambda size: (N, size, width)),
         cross_buf=pltpu.VMEM((block, cols), bf16),
-        grad_out=both(lambda size: (slots, size, emb)),
-        grad_pass=both(lambda size: (2, Y * size, emb)),
-        grad_in=both(lambda size: (2, Y * size, emb)),
+        grad_out=each(lambda size: (slots, size, emb)),
+        grad_pass=each(lambda size: (2, Y * size, emb)),
+        grad_in=each(lambda size: (2, Y * size, emb)),
         row_out=pltpu.VMEM((N, rows_dev, emb), bf16),
         row_in=pltpu.VMEM((N, rows_dev, emb), bf16),
-        load_sem=dma((Z + 4,)), store_sem=dma((2,)), send_sem=dma((64,)),
-        count_sem=dma((2, 2)), row_sem=dma, column_sem=dma((2,)), rank_block_sem=dma((2, 2)),
-        dense_sem=dma((2,)), rank_sem=dma((2,)), ranks_sem=dma((2,)),
-        back_sem=dma((2, 2)), grad_sem=dma((2, 2)), part_sem=dma, sibling_sem=dma,
+        load_sem=dma((Z + 4,)), store_sem=dma((n_parts,)), send_sem=dma((96,)),
+        count_sem=dma((n_parts, 2)), row_sem=dma, column_sem=dma((3,)), rank_block_sem=dma((2, 2)),
+        dense_sem=dma((n_parts,)), rank_sem=dma((n_parts,)), ranks_sem=dma((n_parts,)),
+        back_sem=dma((n_parts, 2)), grad_sem=dma((n_parts, 2)), part_sem=dma, sibling_sem=dma,
     )
     names = (
         "rows_ref", "counts_ref", "state_ref", "down_ref", "up_ref", "bias_ref", "grad_ref",

time: 91.3 us -> 87.4 us (0.957)
  Pallas kernels: 87.3 us -> 83.4 us
    pallas_call x1, Pallas kernels: 87.3 us -> 83.4 us  [on_device(): pl.pallas_call(functools.partial(kernel, n_wide, N, names), out_shape=(ja...]
where the time goes in v4:
time: 87.4 us; the launch traced here: 87.2 us
  Pallas kernels  83.4 us (95%)
  local copies, waits for them, and re-layouts  3.09 us (4%)
    pallas_call x1, Pallas kernels, on_device(): pl.pallas_call(functools.partial(kernel, n_wide, N, names), out_shape=(ja...  83.4 us
    unnamed x2, local copies, waits for them, and re-layouts  3.09 us

profile of v4, /device:TPU:1, one launch (start us, length us, event | category | flops | bytes accessed | tf_op | source)
XLA Modules:
  0.0 87.2 jit_solution(8489879268501467814)
XLA Ops:
  0.6 83.4 %shard_map.86 = (bf16[160,1024]{1,0:T(8,128)(2,1)}, f32[1,64,128]{2,1,0:T(8,128)}) custom-call(bf16[1,64,128]{2,1,0:T(8,128)(2,1)} %refs_0_.1, s32[1,64,10240]{2,1,0:T(8,128)} %refs_1_.1, f32[1,64]{1,0:T(1,128)} %refs_2_.1, bf16[4,16,8192]{2,1,0:T(8,128)(2,1)} %bitcast.3, bf16[4,16,8192]{2,1,0:T(8,128)(2,1)} %bitcast.4, f32[1,8192]{1,0:T(1,128)} %bitcast.5, ...), custom_call_target="tpu_custom_call" | custom-call | tf_op jit(solution)/shard_map/pallas_call | solution.py:479
  84.1 1.7 %copy.11 = bf16[160,1024]{1,0:T(8,128)(2,1)} copy(bf16[160,1024]{1,0:T(8,128)(2,1)} %get-tuple-element.4) | data formatting | bytes 655360
  85.8 1.4 %copy.12 = f32[1,64,128]{2,1,0:T(8,128)} copy(f32[1,64,128]{2,1,0:T(8,128)} %get-tuple-element.5) | data formatting | bytes 65536

commit v5 on v4

--- a/solution.py
+++ b/solution.py
@@ -92,6 +92,33 @@
             wait()
         pending.clear()
 
+    barrier = pltpu.get_barrier_semaphore()
+
+    @pl.loop(1, Y * N)
+    def _(i):
+        to = (y * N + n + i) % (Y * N)
+        pl.semaphore_signal(barrier, inc=1, device_id=(z * Y + to // N, to % N), device_id_type=MESH)
+
+    for step in (1, 2, Z - 2, Z - 1):
+        pl.semaphore_signal(barrier, inc=1, device_id=((z + step) % Z * Y + y, n), device_id_type=MESH)
+
+    for j in range(2):
+        @pl.when(shift(n, j) != 0)
+        def _():
+            to = (z + shift(n, j)) % Z * Y + y
+            pl.semaphore_signal(barrier, inc=1, device_id=(to, n), device_id_type=MESH)
+
+    @pl.loop(0, slots)
+    def _(i):
+        zt, yt = 2 * n + i // Y, i % Y
+        k, _ = unshift((z + Z - zt) % Z)
+
+        @pl.when(jnp.logical_not((zt == z) & (yt == y) & (k == n)))
+        def _():
+            pl.semaphore_signal(barrier, inc=1, device_id=(zt * Y + yt, k), device_id_type=MESH)
+
+    pools_for_itself = jnp.where((shift(n, 1) == 0) & (z // 2 == n), 1, 0)
+
     def load_unit(i, j):
         u = (z + shift((n + 1 + i) % N, j)) % Z
         pltpu.make_async_copy(
@@ -130,33 +157,6 @@
     pl.loop(0, N)(functools.partial(load_unit, j=1))
     for copy in small + fixed:
         copy.start()
-
-    barrier = pltpu.get_barrier_semaphore()
-
-    @pl.loop(1, Y * N)
-    def _(i):
-        to = (y * N + n + i) % (Y * N)
-        pl.semaphore_signal(barrier, inc=1, device_id=(z * Y + to // N, to % N), device_id_type=MESH)
-
-    for step in (1, 2, Z - 2, Z - 1):
-        pl.semaphore_signal(barrier, inc=1, device_id=((z + step) % Z * Y + y, n), device_id_type=MESH)
-
-    for j in range(2):
-        @pl.when(shift(n, j) != 0)
-        def _():
-            to = (z + shift(n, j)) % Z * Y + y
-            pl.semaphore_signal(barrier, inc=1, device_id=(to, n), device_id_type=MESH)
-
-    @pl.loop(0, slots)
-    def _(i):
-        zt, yt = 2 * n + i // Y, i % Y
-        k, _ = unshift((z + Z - zt) % Z)
-
-        @pl.when(jnp.logical_not((zt == z) & (yt == y) & (k == n)))
-        def _():
-            pl.semaphore_signal(barrier, inc=1, device_id=(zt * Y + yt, k), device_id_type=MESH)
-
-    pools_for_itself = jnp.where((shift(n, 1) == 0) & (z // 2 == n), 1, 0)
 
     def code_unit(i, j):
         u = (z + shift((n + 1 + i) % N, j)) % Z

time: 87.4 us -> 86.6 us (level)
  Pallas kernels: 83.4 us -> 82.4 us
    pallas_call x1, Pallas kernels: 83.4 us -> 82.4 us  [on_device(): pl.pallas_call(functools.partial(kernel, n_wide, N, names), out_shape=(ja...]
where the time goes in v5:
time: 86.6 us; the launch traced here: 86.1 us
  Pallas kernels  82.4 us (95%)
  local copies, waits for them, and re-layouts  3.09 us (4%)
    pallas_call x1, Pallas kernels, on_device(): pl.pallas_call(functools.partial(kernel, n_wide, N, names), out_shape=(ja...  82.4 us
    unnamed x2, local copies, waits for them, and re-layouts  3.09 us

profile of v5, /device:TPU:1, one launch (start us, length us, event | category | flops | bytes accessed | tf_op | source)
XLA Modules:
  0.0 86.1 jit_solution(6393233569038636884)
XLA Ops:
  0.6 82.4 %shard_map.86 = (bf16[160,1024]{1,0:T(8,128)(2,1)}, f32[1,64,128]{2,1,0:T(8,128)}) custom-call(bf16[1,64,128]{2,1,0:T(8,128)(2,1)} %refs_0_.1, s32[1,64,10240]{2,1,0:T(8,128)} %refs_1_.1, f32[1,64]{1,0:T(1,128)} %refs_2_.1, bf16[4,16,8192]{2,1,0:T(8,128)(2,1)} %bitcast.3, bf16[4,16,8192]{2,1,0:T(8,128)(2,1)} %bitcast.4, f32[1,8192]{1,0:T(1,128)} %bitcast.5, ...), custom_call_target="tpu_custom_call" | custom-call | tf_op jit(solution)/shard_map/pallas_call | solution.py:479
  83.0 1.7 %copy.11 = bf16[160,1024]{1,0:T(8,128)(2,1)} copy(bf16[160,1024]{1,0:T(8,128)(2,1)} %get-tuple-element.4) | data formatting | bytes 655360
  84.8 1.4 %copy.12 = f32[1,64,128]{2,1,0:T(8,128)} copy(f32[1,64,128]{2,1,0:T(8,128)} %get-tuple-element.5) | data formatting | bytes 65536
